TPU v7x, 512 devices: a whole 4x8x8 slice. The times are simulated.
512 devices in a mesh: ctx: 64 (over y, z_hi, x), head: 8 (over z_lo, core).
Axes of the slice: x: 4, y: 8, z: 8 (z_hi: 2, z_lo: 4; z = z_hi * 4 + z_lo), core: 2. Of those that a mesh axis runs over, the one named last changes fastest.
Arguments:
- queries: bfloat16 [16384, 16384], P('ctx', 'head'), may hold values from -6 to 6
- keys: bfloat16 [16384, 1024], P(('ctx', 'head')), may hold values from -6 to 6
- values: bfloat16 [16384, 1024], P(('ctx', 'head')), may hold values from -0.5390625 to 0.5390625
- out_grad: bfloat16 [16384, 16384], P('ctx', 'head'), may hold values from -96 to 96
- log_norm: float32 [128, 16384], P('head', 'ctx'), as said below
- delta_rows: float32 [128, 16384], P('head', 'ctx'), may hold values from -96 to 96
- doc_start: int32 [16384], P('ctx'), may hold values from 0 to 16383, as said below
Outputs:
- query_grad: bfloat16 [16384, 16384], P('ctx', 'head')
- key_grad: bfloat16 [16384, 1024], P(('ctx', 'head'))
- value_grad: bfloat16 [16384, 1024], P(('ctx', 'head'))
Inputs may be any that keep to these rules, and one draw needn't show every extreme that they name: Documents are contiguous runs of positions; doc_start[p] is the first position of p's document. Each document has 1 to 1024 tokens; one has exactly 1024 tokens and does not begin at a multiple of 256; the last position is a document of its own. log_norm[i, p] lies within 0.5 of 0.5 plus the natural logarithm of p - doc_start[p] + 1.
All inputs are finite; a program needn't handle non-finite values.
Results may differ from a plain program's by a relative error of at most 0.0052.
Values may be sent and summed in bfloat16 or wider, within the bound.
No kernel may reach another device: no remote copies, remote signals or barrier semaphores. Data moves between devices by JAX's collectives and lax.ppermute only.
A program may use at most 64 MiB of HBM per device.

v0:
```python
import jax
import jax.numpy as jnp
from jax import lax
from jax.sharding import PartitionSpec as P

HD = 128
REACH = 4
GROUP_HEADS = 16


def passed_along(block, axis, distance):
    devices = range(lax.axis_size(axis))
    route = [(i - distance, i) for i in devices if i - distance in devices]
    return lax.ppermute(block, axis, route)


def shifted(x, axis, by):
    length = lax.axis_size(axis)
    return lax.ppermute(x, axis, [(i, (i + by) % length) for i in range(length)])


def local(queries, keys, values, out_grad, log_norm, delta_rows, doc_start):
    scale = HD ** (-0.5)
    rows = queries.shape[0]
    width = lax.axis_size("ctx")
    place = lax.axis_index("ctx")
    stacked = jnp.stack([keys, values])
    local_pair = lax.all_to_all(stacked, "head", split_axis=2, concat_axis=1, tiled=True)
    groups = local_pair.shape[2] // HD
    local_pair = local_pair.reshape(2, rows, groups, HD)
    query_local = queries.reshape(rows, groups, GROUP_HEADS, HD)
    grad_local = out_grad.reshape(rows, groups, GROUP_HEADS, HD)
    norm_local = log_norm.reshape(groups, GROUP_HEADS, rows)
    delta_local = delta_rows.reshape(groups, GROUP_HEADS, rows)
    query_pos = place * rows + jnp.arange(rows, dtype=jnp.int32)

    def block_terms(pair_block, base):
        key_pos = base + jnp.arange(rows, dtype=jnp.int32)
        allowed = (key_pos[None, :] >= doc_start[:, None]) & (
            key_pos[None, :] <= query_pos[:, None]
        )

        def compute(unused):
            key_block = pair_block[0]
            value_block = pair_block[1]
            scores = (
                jnp.einsum(
                    "qghd,kgd->ghqk", query_local, key_block, preferred_element_type=jnp.float32
                )
                * scale
            )
            probs = jnp.where(allowed[None, None], jnp.exp(scores - norm_local[..., None]), 0.0)
            probs_b = probs.astype(jnp.bfloat16)
            value_term = jnp.einsum(
                "ghqk,qghd->kgd", probs_b, grad_local, preferred_element_type=jnp.float32
            )
            dprobs = jnp.einsum(
                "qghd,kgd->ghqk", grad_local, value_block, preferred_element_type=jnp.float32
            )
            dscores = (probs * (dprobs - delta_local[..., None])).astype(jnp.bfloat16)
            query_term = (
                jnp.einsum("ghqk,kgd->qghd", dscores, key_block, preferred_element_type=jnp.float32)
                * scale
            )
            key_term = (
                jnp.einsum(
                    "ghqk,qghd->kgd", dscores, query_local, preferred_element_type=jnp.float32
                )
                * scale
            )
            return (query_term, jnp.stack([key_term, value_term]))

        def nothing(unused):
            return (
                jnp.zeros((rows, groups, GROUP_HEADS, HD), jnp.float32),
                jnp.zeros((2, rows, groups, HD), jnp.float32),
            )

        return lax.cond(jnp.any(allowed), compute, nothing, 0)

    query_sum, pair_sum = block_terms(local_pair, place * rows)
    moving = local_pair
    travelling = pair_sum
    for turn in range(1, REACH + 1):
        moving = passed_along(moving, "ctx", 1)
        travelling = shifted(travelling, "ctx", 1)
        query_term, pair_term = block_terms(moving, (place - turn) % width * rows)
        query_sum = query_sum + query_term
        travelling = travelling + pair_term
    pair_sum = shifted(travelling.astype(jnp.bfloat16), "ctx", -REACH).astype(travelling.dtype)
    query_grad = query_sum.astype(jnp.bfloat16).reshape(rows, groups * GROUP_HEADS * HD)
    pair_rounded = pair_sum.astype(jnp.bfloat16).reshape(2, rows, groups * HD)
    returned = lax.all_to_all(pair_rounded, "head", split_axis=1, concat_axis=2, tiled=True)
    return (query_grad, returned[0], returned[1])


def solution(mesh):
    return jax.shard_map(
        local,
        mesh=mesh,
        in_specs=(
            P("ctx", "head"),
            P(("ctx", "head"), None),
            P(("ctx", "head"), None),
            P("ctx", "head"),
            P("head", "ctx"),
            P("head", "ctx"),
            P("ctx"),
        ),
        out_specs=(P("ctx", "head"), P(("ctx", "head"), None), P(("ctx", "head"), None)),
        check_vma=False,
    )
```

profile of v0, /device:TPU:40, one launch (start us, length us, event | category | flops | bytes accessed | tf_op | source)
XLA Modules:
  0.0 190.5 jit_solution(18365478610259750863)
XLA Ops:
  3.2 7.3 %all-to-all-start = ((bf16[8,2,4096]{2,1,0:T(2,128)(2,1)}), bf16[8,2,4096]{2,1,0:T(2,128)(2,1)S(1)}, u32[]{:S(2)}, u32[]{:S(2)}) async-start(bf16[8,2,4096]{2,1,0:T(2,128)(2,1)} %reshape.301), calls=%async_computation | async-start | bytes 262144 | tf_op jit(solution)/shard_map/all_to_all | solution.py:28
  10.5 2.5 %fusion.201 = (pred[]{:T(512)}, pred[]{:T(512)}, pred[]{:T(512)}, pred[]{:T(512)}, pred[]{:T(512)}, /*index=5*/pred[256,256]{0,1:T(8,128)(4,1)}, pred[256,256]{0...) fusion(s32[256]{0:T(256)S(1)} %iota_add_fusion.4, s32[256]{0:T(256)} %param.23, ...), kind=kLoop, calls=%fused_computation.182 | loop fusion | flops 1310715 | bytes 333829 | tf_op jit(solution)/shard_map/reduce_or | solution.py:79
  17.9 5.7 %conditional.5 = (f32[256,1,16,128]{3,0,2,1:T(8,128)S(1)}, f32[2,256,1,128]{3,1,2,0:T(8,128)}) conditional(s32[]{:T(128)} %convert_element_type.53, () %tuple.48, (pred[256,256]{0,1:T(8,128)(4,1)S(1)}, bf16[2,256,1,128]{3,1,2,0:T(8,128)(2,1)S(1)}, bf16[256,1,16,128]{0,3,2,1:T(8,128)(2,1)S(1)}, f32[16,256]{1,0:T(8,128)S(1)}, ...), branch_computations={%region_1.0_spmd, %region_2.3_spmd} | conditional | flops 1353285632 | bytes 30523436 | solution.py:79
  23.7 3.4 %collective-permute-start.4 = (f32[2,256,1,128]{3,1,2,0:T(8,128)}, f32[2,256,1,128]{3,1,2,0:T(8,128)}, u32[]{:S(2)}, u32[]{:S(2)}) collective-permute-start(f32[2,256,1,128]{3,1,2,0:T(8,128)} %get-tuple-element.108), channel_id=1, source_target_pairs={{0,8},{8,16},{16,24},{24,32},{32,40},{40,48},{48,56},{56,64},{64,7... | collective-permute-start | bytes 786440 | tf_op jit(solution)/shard_map/ppermute | solution.py:19
  27.0 3.4 %collective-permute-start = (bf16[2,256,1,128]{3,1,2,0:T(8,128)(2,1)S(1)}, bf16[2,256,1,128]{3,1,2,0:T(8,128)(2,1)S(1)}, u32[]{:S(2)}, u32[]{:S(2)}) collective-permute-start(bf16[2,256,1,128]{3,1,2,0:T(8,128)(2,1)S(1)} %bitcast.541), channel_id=1, source_target_pairs={{0,8},{8,16},{16,24},{24,32},{32,40},{40,48},{48,56},{56,64},{64,7... | collective-permute-start | bytes 393224 | tf_op jit(solution)/shard_map/ppermute | solution.py:14
  31.1 18.9 %collective-permute-done = bf16[2,256,1,128]{3,1,2,0:T(8,128)(2,1)S(1)} collective-permute-done((bf16[2,256,1,128]{3,1,2,0:T(8,128)(2,1)S(1)}, bf16[2,256,1,128]{3,1,2,0:T(8,128)(2,1)S(1)}, u32[]{:S(2)}, u32[]{:S(2)}) %collective-permute-start) | collective-permute-done | bytes 131104 | tf_op jit(solution)/shard_map/ppermute | solution.py:14
  50.0 6.3 %conditional.6 = (f32[256,1,16,128]{3,0,2,1:T(8,128)}, f32[2,256,1,128]{3,1,2,0:T(8,128)S(1)}) conditional(s32[]{:T(128)} %convert_element_type.54, () %tuple.50, (pred[256,256]{0,1:T(8,128)(4,1)}, bf16[2,256,1,128]{3,1,2,0:T(8,128)(2,1)S(1)}, bf16[256,1,16,128]{0,3,2,1:T(8,128)(2,1)S(1)}, f32[16,256]{1,0:T(8,128)S(1)}, ...), branch_computations={%region_4.5_spmd, %region_5.6_spmd} | conditional | flops 1353285632 | bytes 30851172 | solution.py:79
  54.2 2.1 %multiply_bitcast_fusion.1 = f32[256,1,16,128]{3,0,2,1:T(8,128)} fusion(bf16[1,16,256,256]{2,3,1,0:T(8,128)(2,1)S(1)} %fusion.41, bf16[2,256,1,128]{3,1,2,0:T(8,128)(2,1)S(1)} %get-tuple-element.67), kind=kOutput, calls=%fused_computation.45 | convolution fusion | flops 268959744 | bytes 4259840 | tf_op jit(solution)/shard_map/cond/branch_1_fun/ghqk,kgd->qghd/dot_general | solution.py:62
  56.4 1.7 add.115
  58.0 1.9 %collective-permute-start.5 = (f32[2,256,1,128]{3,1,2,0:T(8,128)}, f32[2,256,1,128]{3,1,2,0:T(8,128)}, u32[]{:S(2)}, u32[]{:S(2)}) collective-permute-start(f32[2,256,1,128]{3,1,2,0:T(8,128)} %add.115), channel_id=1, source_target_pairs={{0,8},{8,16},{16,24},{24,32},{32,40},{40,48},{48,56},{56,64},{64,7... | collective-permute-start | bytes 786440 | tf_op jit(solution)/shard_map/ppermute | solution.py:19
  60.0 1.9 %collective-permute-start.1 = (bf16[2,256,1,128]{3,1,2,0:T(8,128)(2,1)S(1)}, bf16[2,256,1,128]{3,1,2,0:T(8,128)(2,1)S(1)}, u32[]{:S(2)}, u32[]{:S(2)}) collective-permute-start(bf16[2,256,1,128]{3,1,2,0:T(8,128)(2,1)S(1)} %collective-permute-done), channel_id=1, source_target_pairs={{0,8},{8,16},{16,24},{24,32},{32,40},{40,48},{48,56},{56,64},{64,7... | collective-permute-start | bytes 393224 | tf_op jit(solution)/shard_map/ppermute | solution.py:14
  62.6 17.1 %collective-permute-done.1 = bf16[2,256,1,128]{3,1,2,0:T(8,128)(2,1)S(1)} collective-permute-done((bf16[2,256,1,128]{3,1,2,0:T(8,128)(2,1)S(1)}, bf16[2,256,1,128]{3,1,2,0:T(8,128)(2,1)S(1)}, u32[]{:S(2)}, u32[]{:S(2)}) %collective-permute-start.1) | collective-permute-done | bytes 131104 | tf_op jit(solution)/shard_map/ppermute | solution.py:14
  81.2 1.7 add.116
  82.9 1.9 %collective-permute-start.6 = (f32[2,256,1,128]{3,1,2,0:T(8,128)}, f32[2,256,1,128]{3,1,2,0:T(8,128)}, u32[]{:S(2)}, u32[]{:S(2)}) collective-permute-start(f32[2,256,1,128]{3,1,2,0:T(8,128)} %add.116), channel_id=1, source_target_pairs={{0,8},{8,16},{16,24},{24,32},{32,40},{40,48},{48,56},{56,64},{64,7... | collective-permute-start | bytes 786440 | tf_op jit(solution)/shard_map/ppermute | solution.py:19
  84.8 1.9 %collective-permute-start.2 = (bf16[2,256,1,128]{3,1,2,0:T(8,128)(2,1)S(1)}, bf16[2,256,1,128]{3,1,2,0:T(8,128)(2,1)}, u32[]{:S(2)}, u32[]{:S(2)}) collective-permute-start(bf16[2,256,1,128]{3,1,2,0:T(8,128)(2,1)S(1)} %collective-permute-done.1), channel_id=1, source_target_pairs={{0,8},{8,16},{16,24},{24,32},{32,40},{40,48},{48,56},{56,64},{64,7... | collective-permute-start | bytes 393224 | tf_op jit(solution)/shard_map/ppermute | solution.py:14
  87.4 13.7 %collective-permute-done.2 = bf16[2,256,1,128]{3,1,2,0:T(8,128)(2,1)} collective-permute-done((bf16[2,256,1,128]{3,1,2,0:T(8,128)(2,1)S(1)}, bf16[2,256,1,128]{3,1,2,0:T(8,128)(2,1)}, u32[]{:S(2)}, u32[]{:S(2)}) %collective-permute-start.2) | collective-permute-done | bytes 131104 | tf_op jit(solution)/shard_map/ppermute | solution.py:14
  102.7 1.7 add.117
  104.4 1.9 %collective-permute-start.7 = (f32[2,256,1,128]{3,1,2,0:T(8,128)}, f32[2,256,1,128]{3,1,2,0:T(8,128)}, u32[]{:S(2)}, u32[]{:S(2)}) collective-permute-start(f32[2,256,1,128]{3,1,2,0:T(8,128)} %add.117), channel_id=1, source_target_pairs={{0,8},{8,16},{16,24},{24,32},{32,40},{40,48},{48,56},{56,64},{64,7... | collective-permute-start | bytes 786440 | tf_op jit(solution)/shard_map/ppermute | solution.py:19
  106.3 3.4 %collective-permute-start.3 = (bf16[2,256,1,128]{3,1,2,0:T(8,128)(2,1)}, bf16[2,256,1,128]{3,1,2,0:T(8,128)(2,1)S(1)}, u32[]{:S(2)}, u32[]{:S(2)}) collective-permute-start(bf16[2,256,1,128]{3,1,2,0:T(8,128)(2,1)} %collective-permute-done.2), channel_id=1, source_target_pairs={{0,8},{8,16},{16,24},{24,32},{32,40},{40,48},{48,56},{56,64},{64,7... | collective-permute-start | bytes 393224 | tf_op jit(solution)/shard_map/ppermute | solution.py:14
  110.4 10.8 %collective-permute-done.3 = bf16[2,256,1,128]{3,1,2,0:T(8,128)(2,1)S(1)} collective-permute-done((bf16[2,256,1,128]{3,1,2,0:T(8,128)(2,1)}, bf16[2,256,1,128]{3,1,2,0:T(8,128)(2,1)S(1)}, u32[]{:S(2)}, u32[]{:S(2)}) %collective-permute-start.3) | collective-permute-done | bytes 131104 | tf_op jit(solution)/shard_map/ppermute | solution.py:14
  123.9 30.5 %collective-permute-start.8 = (bf16[2,256,1,128]{3,1,2,0:T(8,128)(2,1)S(1)}, bf16[2,256,1,128]{3,1,2,0:T(8,128)(2,1)S(1)}, u32[]{:S(2)}, u32[]{:S(2)}) collective-permute-start(bf16[2,256,1,128]{3,1,2,0:T(8,128)(2,1)S(1)} %add_convert_fusion.1), channel_id=1, source_target_pairs={{0,480},{8,488},{16,496},{24,504},{32,0},{40,8},{48,16},{56,24},{6... | collective-permute-start | bytes 393224 | tf_op jit(solution)/shard_map/ppermute | solution.py:19
  154.4 2.5 %collective-permute-done.8 = bf16[2,256,1,128]{3,1,2,0:T(8,128)(2,1)S(1)} collective-permute-done((bf16[2,256,1,128]{3,1,2,0:T(8,128)(2,1)S(1)}, bf16[2,256,1,128]{3,1,2,0:T(8,128)(2,1)S(1)}, u32[]{:S(2)}, u32[]{:S(2)}) %collective-permute-start.8) | collective-permute-done | bytes 131104 | tf_op jit(solution)/shard_map/ppermute | solution.py:19
  157.7 24.4 %all-to-all-start.1 = ((bf16[2,256,128]{2,0,1:T(2,128)(2,1)}), bf16[2,256,128]{2,0,1:T(2,128)(2,1)S(1)}, u32[]{:S(2)}, u32[]{:S(2)}) async-start(bf16[2,256,128]{2,0,1:T(2,128)(2,1)} %copy.113), calls=%async_computation.1 | async-start | bytes 262144 | tf_op jit(solution)/shard_map/all_to_all | solution.py:93
  182.0 4.3 %add_convert_fusion = bf16[256,1,16,128]{3,0,2,1:T(8,128)(2,1)S(1)} fusion(f32[256,1,16,128]{3,0,2,1:T(8,128)} %get-tuple-element.107, f32[256,1,16,128]{3,0,2,1:T(8,128)} %get-tuple-element.106, f32[256,1,16,128]{3,0,2,1:T(8,128)} %get-tuple-element.105, f32[256,1,16,128]{3,0,2,1:T(8,128)S(1)} %get-tuple-element.103, f32[256,1,16,128]{3,0,2,1:T(8,128)} %get-tuple-element.104), kind=kLoop, calls=%fused_computation.165 | loop fusion | flops 2621440 | bytes 11534336 | tf_op jit(solution)/shard_map/convert_element_type | solution.py:91
  (61 shorter events, 32.2 us)
Async XLA Ops:
  0.6 14.5 %copy-start = (bf16[256,2048]{1,0:T(8,128)(2,1)S(1)}, bf16[256,2048]{1,0:T(8,128)(2,1)}, u32[]{:S(2)}) copy-start(bf16[256,2048]{1,0:T(8,128)(2,1)} %param.20) | copy-start | bytes 3145732
  0.6 17.3 %copy-start.11 = (f32[16,256]{1,0:T(8,128)S(1)}, f32[16,256]{1,0:T(8,128)}, u32[]{:S(2)}) copy-start(f32[16,256]{1,0:T(8,128)} %param.22) | copy-start | bytes 49156
  0.7 17.3 %copy-start.10 = (f32[16,256]{1,0:T(8,128)S(1)}, f32[16,256]{1,0:T(8,128)}, u32[]{:S(2)}) copy-start(f32[16,256]{1,0:T(8,128)} %param.21) | copy-start | bytes 49156
  3.2 14.0 %all-to-all-start = ((bf16[8,2,4096]{2,1,0:T(2,128)(2,1)}), bf16[8,2,4096]{2,1,0:T(2,128)(2,1)S(1)}, u32[]{:S(2)}, u32[]{:S(2)}) async-start(bf16[8,2,4096]{2,1,0:T(2,128)(2,1)} %reshape.301), calls=%async_computation | async-start | bytes 262144 | tf_op jit(solution)/shard_map/all_to_all | solution.py:28
  17.9 1.2 copy-start.1
  23.7 32.7 %collective-permute-start.4 = (f32[2,256,1,128]{3,1,2,0:T(8,128)}, f32[2,256,1,128]{3,1,2,0:T(8,128)}, u32[]{:S(2)}, u32[]{:S(2)}) collective-permute-start(f32[2,256,1,128]{3,1,2,0:T(8,128)} %get-tuple-element.108), channel_id=1, source_target_pairs={{0,8},{8,16},{16,24},{24,32},{32,40},{40,48},{48,56},{56,64},{64,7... | collective-permute-start | bytes 786440 | tf_op jit(solution)/shard_map/ppermute | solution.py:19
  27.0 23.0 %collective-permute-start = (bf16[2,256,1,128]{3,1,2,0:T(8,128)(2,1)S(1)}, bf16[2,256,1,128]{3,1,2,0:T(8,128)(2,1)S(1)}, u32[]{:S(2)}, u32[]{:S(2)}) collective-permute-start(bf16[2,256,1,128]{3,1,2,0:T(8,128)(2,1)S(1)} %bitcast.541), channel_id=1, source_target_pairs={{0,8},{8,16},{16,24},{24,32},{32,40},{40,48},{48,56},{56,64},{64,7... | collective-permute-start | bytes 393224 | tf_op jit(solution)/shard_map/ppermute | solution.py:14
  50.0 1.2 copy-start.2
  50.0 1.2 copy-start.9
  51.3 0.8 copy-start.12
  58.0 23.2 %collective-permute-start.5 = (f32[2,256,1,128]{3,1,2,0:T(8,128)}, f32[2,256,1,128]{3,1,2,0:T(8,128)}, u32[]{:S(2)}, u32[]{:S(2)}) collective-permute-start(f32[2,256,1,128]{3,1,2,0:T(8,128)} %add.115), channel_id=1, source_target_pairs={{0,8},{8,16},{16,24},{24,32},{32,40},{40,48},{48,56},{56,64},{64,7... | collective-permute-start | bytes 786440 | tf_op jit(solution)/shard_map/ppermute | solution.py:19
  60.0 19.7 %collective-permute-start.1 = (bf16[2,256,1,128]{3,1,2,0:T(8,128)(2,1)S(1)}, bf16[2,256,1,128]{3,1,2,0:T(8,128)(2,1)S(1)}, u32[]{:S(2)}, u32[]{:S(2)}) collective-permute-start(bf16[2,256,1,128]{3,1,2,0:T(8,128)(2,1)S(1)} %collective-permute-done), channel_id=1, source_target_pairs={{0,8},{8,16},{16,24},{24,32},{32,40},{40,48},{48,56},{56,64},{64,7... | collective-permute-start | bytes 393224 | tf_op jit(solution)/shard_map/ppermute | solution.py:14
  82.9 19.8 %collective-permute-start.6 = (f32[2,256,1,128]{3,1,2,0:T(8,128)}, f32[2,256,1,128]{3,1,2,0:T(8,128)}, u32[]{:S(2)}, u32[]{:S(2)}) collective-permute-start(f32[2,256,1,128]{3,1,2,0:T(8,128)} %add.116), channel_id=1, source_target_pairs={{0,8},{8,16},{16,24},{24,32},{32,40},{40,48},{48,56},{56,64},{64,7... | collective-permute-start | bytes 786440 | tf_op jit(solution)/shard_map/ppermute | solution.py:19
  84.8 16.3 %collective-permute-start.2 = (bf16[2,256,1,128]{3,1,2,0:T(8,128)(2,1)S(1)}, bf16[2,256,1,128]{3,1,2,0:T(8,128)(2,1)}, u32[]{:S(2)}, u32[]{:S(2)}) collective-permute-start(bf16[2,256,1,128]{3,1,2,0:T(8,128)(2,1)S(1)} %collective-permute-done.1), channel_id=1, source_target_pairs={{0,8},{8,16},{16,24},{24,32},{32,40},{40,48},{48,56},{56,64},{64,7... | collective-permute-start | bytes 393224 | tf_op jit(solution)/shard_map/ppermute | solution.py:14
  101.1 20.1 %copy-start.6 = (pred[256,256]{0,1:T(8,128)(4,1)S(1)}, pred[256,256]{0,1:T(8,128)(4,1)}, u32[]{:S(2)}) copy-start(pred[256,256]{0,1:T(8,128)(4,1)} %get-tuple-element.243) | copy-start | bytes 196612
  104.4 18.4 %collective-permute-start.7 = (f32[2,256,1,128]{3,1,2,0:T(8,128)}, f32[2,256,1,128]{3,1,2,0:T(8,128)}, u32[]{:S(2)}, u32[]{:S(2)}) collective-permute-start(f32[2,256,1,128]{3,1,2,0:T(8,128)} %add.117), channel_id=1, source_target_pairs={{0,8},{8,16},{16,24},{24,32},{32,40},{40,48},{48,56},{56,64},{64,7... | collective-permute-start | bytes 786440 | tf_op jit(solution)/shard_map/ppermute | solution.py:19
  106.3 14.9 %collective-permute-start.3 = (bf16[2,256,1,128]{3,1,2,0:T(8,128)(2,1)}, bf16[2,256,1,128]{3,1,2,0:T(8,128)(2,1)S(1)}, u32[]{:S(2)}, u32[]{:S(2)}) collective-permute-start(bf16[2,256,1,128]{3,1,2,0:T(8,128)(2,1)} %collective-permute-done.2), channel_id=1, source_target_pairs={{0,8},{8,16},{16,24},{24,32},{32,40},{40,48},{48,56},{56,64},{64,7... | collective-permute-start | bytes 393224 | tf_op jit(solution)/shard_map/ppermute | solution.py:14
  123.9 33.0 %collective-permute-start.8 = (bf16[2,256,1,128]{3,1,2,0:T(8,128)(2,1)S(1)}, bf16[2,256,1,128]{3,1,2,0:T(8,128)(2,1)S(1)}, u32[]{:S(2)}, u32[]{:S(2)}) collective-permute-start(bf16[2,256,1,128]{3,1,2,0:T(8,128)(2,1)S(1)} %add_convert_fusion.1), channel_id=1, source_target_pairs={{0,480},{8,488},{16,496},{24,504},{32,0},{40,8},{48,16},{56,24},{6... | collective-permute-start | bytes 393224 | tf_op jit(solution)/shard_map/ppermute | solution.py:19
  157.7 31.1 %all-to-all-start.1 = ((bf16[2,256,128]{2,0,1:T(2,128)(2,1)}), bf16[2,256,128]{2,0,1:T(2,128)(2,1)S(1)}, u32[]{:S(2)}, u32[]{:S(2)}) async-start(bf16[2,256,128]{2,0,1:T(2,128)(2,1)} %copy.113), calls=%async_computation.1 | async-start | bytes 262144 | tf_op jit(solution)/shard_map/all_to_all | solution.py:93
where the time goes:
time: 192 us; the launch traced here: 191 us
  starting transfers between devices  81.8 us (43%)
  waiting for transfers between devices  64.4 us (34%)
  local copies, waits for them, and re-layouts  15.2 us (8%)
  other arithmetic  14.5 us (8%)
  matrix products  10.1 us (5%)
  between operations  4.17 us (2%)
    ppermute x4, waiting for transfers between devices, passed_along(): return lax.ppermute(block, axis, route)  60.6 us
    ppermute x5, starting transfers between devices, shifted(): lax.ppermute(x, axis, [(i, (i + by) % length) for i in range(length)])  39.6 us
    all_to_all x1, starting transfers between devices, local(): lax.all_to_all(pair_rounded, 'head', split_axis=1, concat_axis=2, tiled=T...  24.4 us
    ppermute x4, starting transfers between devices, passed_along(): return lax.ppermute(block, axis, route)  10.6 us
    all_to_all x1, starting transfers between devices, local(): lax.all_to_all(stacked, 'head', split_axis=2, concat_axis=1, tiled=True)  7.27 us
    unnamed x15, local copies, waits for them, and re-layouts  6.76 us
    add x3, other arithmetic, local(): travelling = travelling + pair_term  5.07 us
    another operation x6, local copies, waits for them, and re-layouts  4.78 us
  transfers between devices with their start and end apart: 11, of which 7 were waited for; matrix products, arithmetic and copies ran while one was open for 12% of the time, Pallas kernels for 0%

commit v1 on v0

v1 whole, which is shorter than its diff:
```python
import functools
import math

import jax
import jax.numpy as jnp
from jax import lax
from jax.experimental import pallas as pl
from jax.experimental.pallas import tpu as pltpu
from jax.sharding import PartitionSpec as P

HD = 128
ROWS = 256
GROUP_HEADS = 16
HEADS_STEP = 8
HEAD_DEVS = 8
PIECE = ROWS // HEAD_DEVS
ROW_LEN = 4
SCALE = HD ** (-0.5)
LOG2E = math.log2(math.e)
NT = (((1,), (1,)), ((), ()))
F32 = jnp.float32
BF16 = jnp.bfloat16
VMEM_LIMIT = 56 * 2**20


def slot_base(ctx, slot):
    x = ctx % ROW_LEN
    row = ctx // ROW_LEN
    return ((row - jnp.where(slot > x, 1, 0)) * ROW_LEN + slot) * ROWS


def pack_kernel(keys_ref, values_ref, out_ref):
    for h in range(HEAD_DEVS):
        out_ref[h, 0] = keys_ref[:, h * HD : (h + 1) * HD]
        out_ref[h, 1] = values_ref[:, h * HD : (h + 1) * HD]


def unpack_kernel(pair_ref, keys_ref, values_ref):
    for h in range(HEAD_DEVS):
        keys_ref[:, h * HD : (h + 1) * HD] = pair_ref[h, 0]
        values_ref[:, h * HD : (h + 1) * HD] = pair_ref[h, 1]


def attend(ctx, blocks, mask_ref, kt_ref, kv_ref, acc_ref, q_ref, do_ref, ln_ref, dl_ref, ds_ref, emit):
    n = len(blocks)

    @pl.when(pl.program_id(0) == 0)
    def _():
        acc_ref[...] = jnp.zeros_like(acc_ref)
        q_pos = ctx * ROWS + lax.broadcasted_iota(jnp.int32, (1, ROWS), 1)
        for i, (key, value, base) in enumerate(blocks):
            part = slice(i * ROWS, (i + 1) * ROWS)
            k_pos = base + lax.broadcasted_iota(jnp.int32, (ROWS, ROWS), 0)
            allowed = (k_pos >= ds_ref[...]) & (k_pos <= q_pos)
            mask_ref[part] = jnp.where(allowed, jnp.inf, -jnp.inf)
            key = key().reshape(ROWS, HD)
            kv_ref[0, part] = key
            kv_ref[1, part] = value().reshape(ROWS, HD)
            kt_ref[:, part] = key.T

    for h in range(HEADS_STEP):
        col = slice(h * HD, (h + 1) * HD)
        q = q_ref[:, col]
        do = do_ref[:, col]
        scores = lax.dot_general(kv_ref[0], q, NT, preferred_element_type=F32)
        dprobs = lax.dot_general(kv_ref[1], do, NT, preferred_element_type=F32)
        power = scores * (SCALE * LOG2E) - ln_ref[h : h + 1, :] * LOG2E
        probs = jnp.exp2(jnp.minimum(power, mask_ref[...]))
        dscores = (probs * (dprobs - dl_ref[h : h + 1, :])).astype(BF16)
        acc_ref[1] += jnp.dot(probs.astype(BF16), do, preferred_element_type=F32)
        acc_ref[0] += jnp.dot(dscores, q, preferred_element_type=F32)
        emit(col, jnp.dot(kt_ref[...], dscores, preferred_element_type=F32).T)


def near_kernel(ctx_ref, own_ref, prev_ref, q_ref, do_ref, ln_ref, dl_ref, ds_ref,
                dq_ref, grads_ref, acc_ref, mask_ref, kv_ref, kt_ref):
    ctx = ctx_ref[0]
    blocks = [
        (lambda: own_ref[:, 0], lambda: own_ref[:, 1], ctx * ROWS),
        (lambda: prev_ref[:, 0], lambda: prev_ref[:, 1], (ctx - ROW_LEN) * ROWS),
    ]

    def emit(col, value):
        dq_ref[:, col] = value

    attend(ctx, blocks, mask_ref, kt_ref, kv_ref, acc_ref, q_ref, do_ref, ln_ref, dl_ref, ds_ref, emit)

    @pl.when(pl.program_id(0) == pl.num_programs(0) - 1)
    def _():
        for i in range(2):
            part = slice(i * ROWS, (i + 1) * ROWS)
            grads_ref[i, :, 0] = (acc_ref[0, part] * SCALE).reshape(HEAD_DEVS, PIECE, HD)
            grads_ref[i, :, 1] = acc_ref[1, part].reshape(HEAD_DEVS, PIECE, HD)


def rest_kernel(ctx_ref, slots_ref, q_ref, do_ref, ln_ref, dl_ref, ds_ref, dq_near_ref,
                dq_ref, grads_ref, acc_ref, mask_ref, kv_ref, kt_ref):
    ctx = ctx_ref[0]
    x = ctx % ROW_LEN
    slots = [(x + 1 + i) % ROW_LEN for i in range(ROW_LEN - 1)]
    blocks = [
        (lambda s=s: slots_ref[s, :, 0], lambda s=s: slots_ref[s, :, 1], slot_base(ctx, s))
        for s in slots
    ]

    def emit(col, value):
        dq_ref[:, col] = ((value + dq_near_ref[:, col]) * SCALE).astype(BF16)

    attend(ctx, blocks, mask_ref, kt_ref, kv_ref, acc_ref, q_ref, do_ref, ln_ref, dl_ref, ds_ref, emit)

    @pl.when(pl.program_id(0) == pl.num_programs(0) - 1)
    def _():
        grads_ref[x] = jnp.zeros((HEAD_DEVS, 2, PIECE, HD), BF16)
        for i, s in enumerate(slots):
            part = slice(i * ROWS, (i + 1) * ROWS)
            grads_ref[s, :, 0] = (acc_ref[0, part] * SCALE).astype(BF16).reshape(HEAD_DEVS, PIECE, HD)
            grads_ref[s, :, 1] = acc_ref[1, part].astype(BF16).reshape(HEAD_DEVS, PIECE, HD)


def attention_call(kernel, count, extra_in, dq_type, grads, name):
    def whole(shape):
        return pl.BlockSpec(shape, lambda g: (0,) * len(shape))

    wide = pl.BlockSpec((ROWS, HEADS_STEP * HD), lambda g: (0, g))
    stat = pl.BlockSpec((HEADS_STEP, ROWS), lambda g: (g, 0))
    block = (HEAD_DEVS, 2, PIECE, HD)
    block_specs = [whole(block)] * 2 if count == 2 else [whole((ROW_LEN, *block))]
    return pl.pallas_call(
        kernel,
        grid=(GROUP_HEADS // HEADS_STEP,),
        out_shape=(jax.ShapeDtypeStruct((ROWS, GROUP_HEADS * HD), dq_type), grads),
        in_specs=[pl.BlockSpec(memory_space=pltpu.SMEM), *block_specs, wide, wide, stat, stat,
                  whole((1, ROWS))] + [wide] * extra_in,
        out_specs=(wide, whole(grads.shape)),
        scratch_shapes=[
            pltpu.VMEM((2, count * ROWS, HD), F32),
            pltpu.VMEM((count * ROWS, ROWS), F32),
            pltpu.VMEM((2, count * ROWS, HD), BF16),
            pltpu.VMEM((HD, count * ROWS), BF16),
        ],
        compiler_params=pltpu.CompilerParams(vmem_limit_bytes=VMEM_LIMIT),
        name=name,
    )


def gather_kernel(ctx_ref, back_ref, near_ref, own_ref, prev_ref):
    x = ctx_ref[0] % ROW_LEN
    own = near_ref[0]
    prev = near_ref[1]
    for s in range(ROW_LEN):
        term = back_ref[s].astype(F32)
        own = own + jnp.where(s > x, term, 0.0)
        prev = prev + jnp.where(s < x, term, 0.0)
    own_ref[...] = own
    prev_ref[...] = prev.astype(BF16)


def local(width, queries, keys, values, out_grad, log_norm, delta_rows, doc_start):
    ctx = lax.axis_index("ctx").astype(jnp.int32)
    x = ctx % ROW_LEN
    ctx_arr = ctx.reshape(1)
    first = doc_start.reshape(1, ROWS)
    block = (HEAD_DEVS, 2, PIECE, HD)
    rows = [[r * ROW_LEN + s for s in range(ROW_LEN)] for r in range(width // ROW_LEN)]
    up = [(i, i + ROW_LEN) for i in range(width - ROW_LEN)]
    down = [(i + ROW_LEN, i) for i in range(width - ROW_LEN)]

    packed = pl.pallas_call(pack_kernel, out_shape=jax.ShapeDtypeStruct(block, BF16), name="pack")(keys, values)
    own = lax.all_to_all(packed, "head", split_axis=0, concat_axis=0, tiled=True)
    prev = lax.ppermute(own, "ctx", up)
    slot = lax.broadcasted_iota(jnp.int32, (ROW_LEN, 1, 1, 1, 1), 0)
    outgoing = jnp.where(slot > x, own[None], prev[None])
    slots = lax.all_to_all(outgoing, "ctx", split_axis=0, concat_axis=0, tiled=True, axis_index_groups=rows)

    dq_near, near = attention_call(
        near_kernel, 2, 0, F32, jax.ShapeDtypeStruct((2, *block), F32), "near"
    )(ctx_arr, own, prev, queries, out_grad, log_norm, delta_rows, first)
    query_grad, rest = attention_call(
        rest_kernel, 3, 1, BF16, jax.ShapeDtypeStruct((ROW_LEN, *block), BF16), "rest"
    )(ctx_arr, slots, queries, out_grad, log_norm, delta_rows, first, dq_near)

    back = lax.all_to_all(rest, "ctx", split_axis=0, concat_axis=0, tiled=True, axis_index_groups=rows)
    own_sum, prev_sum = pl.pallas_call(
        gather_kernel,
        in_specs=[pl.BlockSpec(memory_space=pltpu.SMEM)] + [pl.BlockSpec(memory_space=pltpu.VMEM)] * 2,
        out_shape=(jax.ShapeDtypeStruct(block, F32), jax.ShapeDtypeStruct(block, BF16)),
        name="gather",
    )(ctx_arr, back, near)
    from_next = lax.ppermute(prev_sum, "ctx", down)
    total = (own_sum + from_next.astype(F32)).astype(BF16)
    returned = lax.all_to_all(total, "head", split_axis=0, concat_axis=0, tiled=True)
    key_grad, value_grad = pl.pallas_call(
        unpack_kernel,
        out_shape=(jax.ShapeDtypeStruct((PIECE, HEAD_DEVS * HD), BF16),) * 2,
        name="unpack",
    )(returned)
    return query_grad, key_grad, value_grad


def solution(mesh):
    return jax.shard_map(
        functools.partial(local, mesh.shape["ctx"]),
        mesh=mesh,
        in_specs=(
            P("ctx", "head"),
            P(("ctx", "head"), None),
            P(("ctx", "head"), None),
            P("ctx", "head"),
            P("head", "ctx"),
            P("head", "ctx"),
            P("ctx"),
        ),
        out_specs=(P("ctx", "head"), P(("ctx", "head"), None), P(("ctx", "head"), None)),
        check_vma=False,
    )
```

time: 192 us -> 97 us (0.51)
  the two profiles are of different devices: /device:TPU:40 before, /device:TPU:48 now
where the time goes in v1:
time: 97 us; the launch traced here: 96.5 us
  blocking collectives  39.7 us (41%)
  Pallas kernels  24.8 us (26%)
  starting transfers between devices  20.6 us (21%)
  waiting for transfers between devices  8.05 us (8%)
  other arithmetic  1.89 us (2%)
    all_to_all x1, blocking collectives, local(): lax.all_to_all(packed, 'head', split_axis=0, concat_axis=0, tiled=True)  14 us
    all_to_all x1, blocking collectives, local(): lax.all_to_all(rest, 'ctx', split_axis=0, concat_axis=0, tiled=True, axis...  13 us
    all_to_all x1, blocking collectives, local(): lax.all_to_all(total, 'head', split_axis=0, concat_axis=0, tiled=True)  12.7 us
    pallas_call x1, Pallas kernels, local(): attention_call(rest_kernel, 3, 1, BF16, jax.ShapeDtypeStruct((ROW_LEN, *b...  11.2 us
    pallas_call x1, Pallas kernels, local(): attention_call(near_kernel, 2, 0, F32, jax.ShapeDtypeStruct((2, *block),...  8.43 us
    ppermute x1, starting transfers between devices, local(): prev = lax.ppermute(own, 'ctx', up)  8.21 us
    ppermute x1, starting transfers between devices, local(): from_next = lax.ppermute(prev_sum, 'ctx', down)  8.08 us
    ppermute x1, waiting for transfers between devices, local(): prev = lax.ppermute(own, 'ctx', up)  5.17 us
  transfers between devices with their start and end apart: 3, of which 2 were waited for; matrix products, arithmetic and copies ran while one was open for 0% of the time, Pallas kernels for 9%

profile of v1, /device:TPU:48, one launch (start us, length us, event | category | flops | bytes accessed | tf_op | source)
XLA Modules:
  0.0 96.5 jit_solution(4353358482258429694)
XLA Ops:
  0.6 1.6 %pack.1 = bf16[8,2,32,128]{3,2,1,0:T(8,128)(2,1)} custom-call(bf16[32,1024]{1,0:T(8,128)(2,1)} %keys_ref.1, bf16[32,1024]{1,0:T(8,128)(2,1)} %values_ref.1), custom_call_target="tpu_custom_call" | custom-call | tf_op jit(solution)/shard_map/pack/pallas_call | solution.py:168
  2.2 14.0 %all_to_all.20.own_ref = bf16[8,2,32,128]{3,2,1,0:T(8,128)(2,1)S(1)} all-to-all(bf16[8,2,32,128]{3,2,1,0:T(8,128)(2,1)} %pack.1), channel_id=1, replica_groups=mesh['ctx'=64,'head'=8] {'head'}, dimensions={0} | all-to-all | bytes 262144 | tf_op jit(solution)/shard_map/all_to_all | solution.py:169
  16.2 0.0 copy-start.1
  16.2 8.2 %collective-permute-start = (bf16[8,2,32,128]{3,2,1,0:T(8,128)(2,1)S(1)}, bf16[8,2,32,128]{3,2,1,0:T(8,128)(2,1)S(1)}, u32[]{:S(2)}, u32[]{:S(2)}) collective-permute-start(bf16[8,2,32,128]{3,2,1,0:T(8,128)(2,1)S(1)} %all_to_all.20.own_ref), channel_id=1, source_target_pairs={{0,32},{8,40},{16,48},{24,56},{32,64},{40,72},{48,80},{56,88},{64,... | collective-permute-start | bytes 393224 | tf_op jit(solution)/shard_map/ppermute | solution.py:170
  24.5 5.2 %collective-permute-done.prev_ref = bf16[8,2,32,128]{3,2,1,0:T(8,128)(2,1)S(1)} collective-permute-done((bf16[8,2,32,128]{3,2,1,0:T(8,128)(2,1)S(1)}, bf16[8,2,32,128]{3,2,1,0:T(8,128)(2,1)S(1)}, u32[]{:S(2)}, u32[]{:S(2)}) %collective-permute-start) | collective-permute-done | bytes 131104 | tf_op jit(solution)/shard_map/ppermute | solution.py:170
  29.6 0.0 copy-start.2
  29.6 0.9 broadcast_select_fusion
  30.5 4.3 %all-to-all-start.1 = ((bf16[4,8,2,32,128]{4,3,2,1,0:T(8,128)(2,1)}), bf16[4,8,2,32,128]{4,3,2,1,0:T(8,128)(2,1)S(1)}, u32[]{:S(2)}, u32[]{:S(2)}) async-start(bf16[4,8,2,32,128]{4,3,2,1,0:T(8,128)(2,1)} %broadcast_select_fusion), calls=%async_computation.1 | async-start | bytes 1048576 | tf_op jit(solution)/shard_map/all_to_all | solution.py:173
  34.8 0.0 copy-done.1
  34.8 0.0 copy-done.2
  34.8 8.4 %near.1 = (f32[256,2048]{1,0:T(8,128)}, f32[2,8,2,32,128]{4,3,2,1,0:T(8,128)}) custom-call(s32[1]{0:T(128)} %bitcast.ctx_ref, bf16[8,2,32,128]{3,2,1,0:T(8,128)(2,1)} %copy-done.1, bf16[8,2,32,128]{3,2,1,0:T(8,128)(2,1)} %copy-done.2, bf16[256,2048]{1,0:T(8,128)(2,1)} %q_ref.3, bf16[256,2048]{1,0:T(8,128)(2,1)} %do_ref.3, f32[16,256]{1,0:T(8,128)} %ln_ref.3, ...), custom_call_target="tpu_custom_call" | custom-call | tf_op jit(solution)/shard_map/near/pallas_call | solution.py:175
  43.3 0.0 all-to-all-done.1.slots_ref
  43.3 0.0 copy-start
  43.3 0.8 copy-done
  44.1 11.2 %rest.1 = (bf16[256,2048]{1,0:T(8,128)(2,1)}, bf16[4,8,2,32,128]{4,3,2,1,0:T(8,128)(2,1)}) custom-call(s32[1]{0:T(128)} %bitcast.ctx_ref, bf16[4,8,2,32,128]{4,3,2,1,0:T(8,128)(2,1)} %copy-done, bf16[256,2048]{1,0:T(8,128)(2,1)} %q_ref.3, bf16[256,2048]{1,0:T(8,128)(2,1)} %do_ref.3, f32[16,256]{1,0:T(8,128)} %ln_ref.3, f32[16,256]{1,0:T(8,128)} %dl_ref.3, ...), custom_call_target="tpu_custom_call" | custom-call | tf_op jit(solution)/shard_map/rest/pallas_call | solution.py:178
  55.3 13.0 %all_to_all.21.back_ref = bf16[4,8,2,32,128]{4,3,2,1,0:T(8,128)(2,1)} all-to-all(bf16[4,8,2,32,128]{4,3,2,1,0:T(8,128)(2,1)} %get-tuple-element.13), channel_id=1, replica_groups={{0,8,16,24},{32,40,48,56},{64,72,80,88},{96,104,112,120},{128,136,144,1..., dimensions={0} | all-to-all | bytes 1048576 | tf_op jit(solution)/shard_map/all_to_all | solution.py:182
  68.2 2.1 %gather.1 = (f32[8,2,32,128]{3,2,1,0:T(8,128)}, bf16[8,2,32,128]{3,2,1,0:T(8,128)(2,1)}) custom-call(s32[1]{0:T(128)} %bitcast.ctx_ref, bf16[4,8,2,32,128]{4,3,2,1,0:T(8,128)(2,1)} %all_to_all.21.back_ref, f32[2,8,2,32,128]{4,3,2,1,0:T(8,128)} %get-tuple-element.14.near_ref), custom_call_target="tpu_custom_call" | custom-call | tf_op jit(solution)/shard_map/gather/pallas_call | solution.py:183
  70.3 8.1 %collective-permute-start.1 = (bf16[8,2,32,128]{3,2,1,0:T(8,128)(2,1)}, bf16[8,2,32,128]{3,2,1,0:T(8,128)(2,1)S(1)}, u32[]{:S(2)}, u32[]{:S(2)}) collective-permute-start(bf16[8,2,32,128]{3,2,1,0:T(8,128)(2,1)} %get-tuple-element.16), channel_id=1, source_target_pairs={{32,0},{40,8},{48,16},{56,24},{64,32},{72,40},{80,48},{88,56},{96,... | collective-permute-start | bytes 393224 | tf_op jit(solution)/shard_map/ppermute | solution.py:189
  78.4 2.9 %collective-permute-done.1 = bf16[8,2,32,128]{3,2,1,0:T(8,128)(2,1)S(1)} collective-permute-done((bf16[8,2,32,128]{3,2,1,0:T(8,128)(2,1)}, bf16[8,2,32,128]{3,2,1,0:T(8,128)(2,1)S(1)}, u32[]{:S(2)}, u32[]{:S(2)}) %collective-permute-start.1) | collective-permute-done | bytes 131104 | tf_op jit(solution)/shard_map/ppermute | solution.py:189
  81.3 1.0 %add_convert_fusion = bf16[8,2,32,128]{3,2,1,0:T(8,128)(2,1)S(1)} fusion(f32[8,2,32,128]{3,2,1,0:T(8,128)} %get-tuple-element.15, bf16[8,2,32,128]{3,2,1,0:T(8,128)(2,1)S(1)} %collective-permute-done.1), kind=kLoop, calls=%fused_computation.1 | loop fusion | flops 196608 | bytes 524288 | tf_op jit(solution)/shard_map/convert_element_type | solution.py:190
  82.3 12.7 %all_to_all.22.pair_ref = bf16[8,2,32,128]{3,2,1,0:T(8,128)(2,1)} all-to-all(bf16[8,2,32,128]{3,2,1,0:T(8,128)(2,1)S(1)} %add_convert_fusion), channel_id=1, replica_groups=mesh['ctx'=64,'head'=8] {'head'}, dimensions={0} | all-to-all | bytes 262144 | tf_op jit(solution)/shard_map/all_to_all | solution.py:191
  94.9 1.6 %unpack.1 = (bf16[32,1024]{1,0:T(8,128)(2,1)}, bf16[32,1024]{1,0:T(8,128)(2,1)}) custom-call(bf16[8,2,32,128]{3,2,1,0:T(8,128)(2,1)} %all_to_all.22.pair_ref), custom_call_target="tpu_custom_call" | custom-call | tf_op jit(solution)/shard_map/unpack/pallas_call | solution.py:192
  (1 shorter events, 0.0 us)
Async XLA Ops:
  16.2 18.6 %copy-start.1 = (bf16[8,2,32,128]{3,2,1,0:T(8,128)(2,1)}, bf16[8,2,32,128]{3,2,1,0:T(8,128)(2,1)S(1)}, u32[]{:S(2)}) copy-start(bf16[8,2,32,128]{3,2,1,0:T(8,128)(2,1)S(1)} %all_to_all.20.own_ref) | copy-start | bytes 393220
  16.2 13.4 %collective-permute-start = (bf16[8,2,32,128]{3,2,1,0:T(8,128)(2,1)S(1)}, bf16[8,2,32,128]{3,2,1,0:T(8,128)(2,1)S(1)}, u32[]{:S(2)}, u32[]{:S(2)}) collective-permute-start(bf16[8,2,32,128]{3,2,1,0:T(8,128)(2,1)S(1)} %all_to_all.20.own_ref), channel_id=1, source_target_pairs={{0,32},{8,40},{16,48},{24,56},{32,64},{40,72},{48,80},{56,88},{64,... | collective-permute-start | bytes 393224 | tf_op jit(solution)/shard_map/ppermute | solution.py:170
  29.6 5.2 %copy-start.2 = (bf16[8,2,32,128]{3,2,1,0:T(8,128)(2,1)}, bf16[8,2,32,128]{3,2,1,0:T(8,128)(2,1)S(1)}, u32[]{:S(2)}) copy-start(bf16[8,2,32,128]{3,2,1,0:T(8,128)(2,1)S(1)} %collective-permute-done.prev_ref) | copy-start | bytes 393220
  30.5 12.7 %all-to-all-start.1 = ((bf16[4,8,2,32,128]{4,3,2,1,0:T(8,128)(2,1)}), bf16[4,8,2,32,128]{4,3,2,1,0:T(8,128)(2,1)S(1)}, u32[]{:S(2)}, u32[]{:S(2)}) async-start(bf16[4,8,2,32,128]{4,3,2,1,0:T(8,128)(2,1)} %broadcast_select_fusion), calls=%async_computation.1 | async-start | bytes 1048576 | tf_op jit(solution)/shard_map/all_to_all | solution.py:173
  43.3 0.8 copy-start
  70.3 11.0 %collective-permute-start.1 = (bf16[8,2,32,128]{3,2,1,0:T(8,128)(2,1)}, bf16[8,2,32,128]{3,2,1,0:T(8,128)(2,1)S(1)}, u32[]{:S(2)}, u32[]{:S(2)}) collective-permute-start(bf16[8,2,32,128]{3,2,1,0:T(8,128)(2,1)} %get-tuple-element.16), channel_id=1, source_target_pairs={{32,0},{40,8},{48,16},{56,24},{64,32},{72,40},{80,48},{88,56},{96,... | collective-permute-start | bytes 393224 | tf_op jit(solution)/shard_map/ppermute | solution.py:189

commit v2 on v1

v2 whole, which is shorter than its diff:
```python
import functools
import math

import jax
import jax.numpy as jnp
from jax import lax
from jax.experimental import pallas as pl
from jax.experimental.pallas import tpu as pltpu
from jax.sharding import PartitionSpec as P

HD = 128
ROWS = 256
GROUP_HEADS = 16
HEAD_DEVS = 8
PIECE = ROWS // HEAD_DEVS
ROW_LEN = 4
SCALE = HD ** (-0.5)
LOG2E = math.log2(math.e)
NT = (((1,), (1,)), ((), ()))
F32 = jnp.float32
BF16 = jnp.bfloat16
VMEM_LIMIT = 14 * 2**20


def slot_base(ctx, slot):
    x = ctx % ROW_LEN
    row = ctx // ROW_LEN
    return ((row - jnp.where(slot > x, 1, 0)) * ROW_LEN + slot) * ROWS


def pack_kernel(keys_ref, values_ref, out_ref):
    for h in range(HEAD_DEVS):
        out_ref[h, 0] = keys_ref[:, h * HD : (h + 1) * HD]
        out_ref[h, 1] = values_ref[:, h * HD : (h + 1) * HD]


def unpack_kernel(pair_ref, keys_ref, values_ref):
    for h in range(HEAD_DEVS):
        keys_ref[:, h * HD : (h + 1) * HD] = pair_ref[h, 0]
        values_ref[:, h * HD : (h + 1) * HD] = pair_ref[h, 1]


def attend(ctx, blocks, mask_ref, kt_ref, kv_ref, acc_ref, q_ref, do_ref, ln_ref, dl_ref, ds_ref, emit):
    q_pos = ctx * ROWS + lax.broadcasted_iota(jnp.int32, (1, ROWS), 1)
    for i, (ref, base) in enumerate(blocks):
        part = slice(i * ROWS, (i + 1) * ROWS)
        k_pos = base + lax.broadcasted_iota(jnp.int32, (ROWS, ROWS), 0)
        allowed = (k_pos >= ds_ref[...]) & (k_pos <= q_pos)
        mask_ref[part] = jnp.where(allowed, jnp.inf, -jnp.inf)
        key = ref[:, 0].reshape(ROWS, HD)
        kv_ref[0, part] = key
        kv_ref[1, part] = ref[:, 1].reshape(ROWS, HD)
        kt_ref[:, part] = key.T

    for h in range(GROUP_HEADS):
        col = slice(h * HD, (h + 1) * HD)
        q = q_ref[:, col]
        do = do_ref[:, col]
        scores = lax.dot_general(kv_ref[0], q, NT, preferred_element_type=F32)
        dprobs = lax.dot_general(kv_ref[1], do, NT, preferred_element_type=F32)
        power = scores * (SCALE * LOG2E) - ln_ref[h : h + 1, :] * LOG2E
        probs = jnp.exp2(jnp.minimum(power, mask_ref[...]))
        dscores = (probs * (dprobs - dl_ref[h : h + 1, :])).astype(BF16)
        value_term = jnp.dot(probs.astype(BF16), do, preferred_element_type=F32)
        key_term = jnp.dot(dscores, q, preferred_element_type=F32)
        if h:
            value_term += acc_ref[1]
            key_term += acc_ref[0]
        acc_ref[1] = value_term
        acc_ref[0] = key_term
        emit(col, jnp.dot(kt_ref[...], dscores, preferred_element_type=F32).T)


def put_grads(ref, acc_ref, part):
    ref[:, 0] = (acc_ref[0, part] * SCALE).astype(ref.dtype).reshape(HEAD_DEVS, PIECE, HD)
    ref[:, 1] = acc_ref[1, part].astype(ref.dtype).reshape(HEAD_DEVS, PIECE, HD)


def one_kernel(offset, ctx_ref, block_ref, q_ref, do_ref, ln_ref, dl_ref, ds_ref,
               dq_ref, grads_ref, acc_ref, mask_ref, kv_ref, kt_ref):
    ctx = ctx_ref[0]

    def emit(col, value):
        dq_ref[:, col] = value.astype(BF16)

    attend(ctx, [(block_ref, (ctx - offset) * ROWS)], mask_ref, kt_ref, kv_ref, acc_ref, q_ref, do_ref, ln_ref, dl_ref, ds_ref, emit)
    put_grads(grads_ref, acc_ref, slice(None))


def rest_kernel(ctx_ref, slots_ref, q_ref, do_ref, ln_ref, dl_ref, ds_ref,
                dq_ref, grads_ref, acc_ref, mask_ref, kv_ref, kt_ref):
    ctx = ctx_ref[0]
    x = ctx % ROW_LEN
    slots = [(x + 1 + i) % ROW_LEN for i in range(ROW_LEN - 1)]

    def emit(col, value):
        dq_ref[:, col] = value.astype(BF16)

    blocks = [(slots_ref.at[s], slot_base(ctx, s)) for s in slots]
    attend(ctx, blocks, mask_ref, kt_ref, kv_ref, acc_ref, q_ref, do_ref, ln_ref, dl_ref, ds_ref, emit)
    grads_ref[x] = jnp.zeros((HEAD_DEVS, 2, PIECE, HD), BF16)
    for i, s in enumerate(slots):
        put_grads(grads_ref.at[s], acc_ref, slice(i * ROWS, (i + 1) * ROWS))


def vmem_call(kernel, out, *args, name, scratch=()):
    specs = [pl.BlockSpec(memory_space=pltpu.SMEM if a.size == 1 else pltpu.VMEM) for a in args]
    outs = jax.tree.map(lambda _: pl.BlockSpec(memory_space=pltpu.VMEM), out)
    return pl.pallas_call(
        kernel,
        out_shape=out,
        in_specs=specs,
        out_specs=outs,
        scratch_shapes=scratch,
        compiler_params=pltpu.CompilerParams(vmem_limit_bytes=VMEM_LIMIT),
        name=name,
    )(*args)


def attention_call(kernel, count, grads, name, *args):
    scratch = [
        pltpu.VMEM((2, count * ROWS, HD), F32),
        pltpu.VMEM((count * ROWS, ROWS), F32),
        pltpu.VMEM((2, count * ROWS, HD), BF16),
        pltpu.VMEM((HD, count * ROWS), BF16),
    ]
    dq = jax.ShapeDtypeStruct((ROWS, GROUP_HEADS * HD), BF16)
    return vmem_call(kernel, (dq, grads), *args, name=name, scratch=scratch)


def prev_sum_kernel(ctx_ref, back_ref, near_ref, out_ref):
    x = ctx_ref[0] % ROW_LEN
    total = near_ref[...]
    for s in range(ROW_LEN):
        total = total + jnp.where(s < x, back_ref[s].astype(F32), 0.0)
    out_ref[...] = total.astype(BF16)


def own_sum_kernel(ctx_ref, back_ref, near_ref, out_ref):
    x = ctx_ref[0] % ROW_LEN
    total = near_ref[...]
    for s in range(ROW_LEN):
        total = total + jnp.where(s > x, back_ref[s].astype(F32), 0.0)
    out_ref[...] = total


def add_kernel(a_ref, b_ref, out_ref):
    out_ref[...] = (a_ref[...] + b_ref[...].astype(F32)).astype(BF16)


def local(width, queries, keys, values, out_grad, log_norm, delta_rows, doc_start):
    ctx = lax.axis_index("ctx").astype(jnp.int32)
    x = ctx % ROW_LEN
    ctx_arr = ctx.reshape(1)
    first = doc_start.reshape(1, ROWS)
    block = (HEAD_DEVS, 2, PIECE, HD)
    rows = [[r * ROW_LEN + s for s in range(ROW_LEN)] for r in range(width // ROW_LEN)]
    up = [(i, i + ROW_LEN) for i in range(width - ROW_LEN)]
    down = [(i + ROW_LEN, i) for i in range(width - ROW_LEN)]

    pieces = jax.ShapeDtypeStruct(block, BF16)
    pieces_f32 = jax.ShapeDtypeStruct(block, F32)
    slots_type = jax.ShapeDtypeStruct((ROW_LEN, *block), BF16)
    side = (queries, out_grad, log_norm, delta_rows, first)

    packed = pl.pallas_call(pack_kernel, out_shape=pieces, name="pack")(keys, values)
    own = lax.all_to_all(packed, "head", split_axis=0, concat_axis=0, tiled=True)
    prev = lax.ppermute(own, "ctx", up)
    slot = lax.broadcasted_iota(jnp.int32, (ROW_LEN, 1, 1, 1, 1), 0)
    outgoing = jnp.where(slot > x, own[None], prev[None])
    slots = lax.all_to_all(outgoing, "ctx", split_axis=0, concat_axis=0, tiled=True, axis_index_groups=rows)
    dq_own, own_grads = attention_call(
        functools.partial(one_kernel, 0), 1, pieces_f32, "own", ctx_arr, own, *side
    )
    slots, dq_own = lax.optimization_barrier((slots, dq_own))
    dq_rest, rest = attention_call(rest_kernel, 3, slots_type, "rest", ctx_arr, slots, *side)

    rest, prev = lax.optimization_barrier((rest, prev))
    back = lax.all_to_all(rest, "ctx", split_axis=0, concat_axis=0, tiled=True, axis_index_groups=rows)
    dq_prev, prev_grads = attention_call(
        functools.partial(one_kernel, ROW_LEN), 1, pieces_f32, "prev", ctx_arr, prev, *side
    )
    query_grad = (dq_own.astype(F32) + dq_rest.astype(F32) + dq_prev.astype(F32)) * SCALE
    query_grad = query_grad.astype(BF16)
    prev_sum = vmem_call(prev_sum_kernel, pieces, ctx_arr, back, prev_grads, name="prev_sum")
    from_next = lax.ppermute(prev_sum, "ctx", down)
    own_sum = vmem_call(own_sum_kernel, pieces_f32, ctx_arr, back, own_grads, name="own_sum")
    total = vmem_call(add_kernel, pieces, own_sum, from_next, name="add")
    returned = lax.all_to_all(total, "head", split_axis=0, concat_axis=0, tiled=True)
    tokens = jax.ShapeDtypeStruct((PIECE, HEAD_DEVS * HD), BF16)
    key_grad, value_grad = vmem_call(unpack_kernel, (tokens, tokens), returned, name="unpack")
    return query_grad, key_grad, value_grad


def solution(mesh):
    return jax.shard_map(
        functools.partial(local, mesh.shape["ctx"]),
        mesh=mesh,
        in_specs=(
            P("ctx", "head"),
            P(("ctx", "head"), None),
            P(("ctx", "head"), None),
            P("ctx", "head"),
            P("head", "ctx"),
            P("head", "ctx"),
            P("ctx"),
        ),
        out_specs=(P("ctx", "head"), P(("ctx", "head"), None), P(("ctx", "head"), None)),
        check_vma=False,
    )
```

time: 97 us -> 90.1 us (0.929)
  the two profiles are of different devices: /device:TPU:48 before, /device:TPU:40 now
where the time goes in v2:
time: 90.1 us; the launch traced here: 89.5 us
  starting transfers between devices  30.8 us (34%)
  Pallas kernels  19.7 us (22%)
  waiting for transfers between devices  17.5 us (19%)
  blocking collectives  14.2 us (16%)
  other arithmetic  3.62 us (4%)
  local copies, waits for them, and re-layouts  2.95 us (3%)
    pallas_call x7, Pallas kernels, vmem_call(): pl.pallas_call(kernel, out_shape=out, in_specs=specs, out_specs=outs, scr...  18.1 us
    all_to_all x1, blocking collectives, local(): lax.all_to_all(packed, 'head', split_axis=0, concat_axis=0, tiled=True)  14.2 us
    ppermute x1, starting transfers between devices, local(): from_next = lax.ppermute(prev_sum, 'ctx', down)  9.84 us
    ppermute x1, starting transfers between devices, local(): prev = lax.ppermute(own, 'ctx', up)  8.21 us
    ppermute x1, waiting for transfers between devices, local(): prev = lax.ppermute(own, 'ctx', up)  5.17 us
    all_to_all x1, starting transfers between devices, local(): lax.all_to_all(total, 'head', split_axis=0, concat_axis=0, tiled=True)  4.85 us
    all_to_all x1, starting transfers between devices, local(): lax.all_to_all(outgoing, 'ctx', split_axis=0, concat_axis=0, tiled=True,...  4.29 us
    all_to_all x1, waiting for transfers between devices, local(): lax.all_to_all(total, 'head', split_axis=0, concat_axis=0, tiled=True)  4.05 us
  transfers between devices with their start and end apart: 5, of which 5 were waited for; matrix products, arithmetic and copies ran while one was open for 3% of the time, Pallas kernels for 9%

profile of v2, /device:TPU:40, one launch (start us, length us, event | category | flops | bytes accessed | tf_op | source)
XLA Modules:
  0.0 89.5 jit_solution(11811108336278661933)
XLA Ops:
  0.6 1.6 %pack.1 = bf16[8,2,32,128]{3,2,1,0:T(8,128)(2,1)} custom-call(bf16[32,1024]{1,0:T(8,128)(2,1)} %keys_ref.1, bf16[32,1024]{1,0:T(8,128)(2,1)} %values_ref.1), custom_call_target="tpu_custom_call" | custom-call | tf_op jit(solution)/shard_map/pack/pallas_call | solution.py:166
  2.2 14.2 %all_to_all.20.block_ref = bf16[8,2,32,128]{3,2,1,0:T(8,128)(2,1)S(1)} all-to-all(bf16[8,2,32,128]{3,2,1,0:T(8,128)(2,1)} %pack.1), channel_id=1, replica_groups=mesh['ctx'=64,'head'=8] {'head'}, dimensions={0} | all-to-all | bytes 262144 | tf_op jit(solution)/shard_map/all_to_all | solution.py:167
  16.4 8.2 %collective-permute-start = (bf16[8,2,32,128]{3,2,1,0:T(8,128)(2,1)S(1)}, bf16[8,2,32,128]{3,2,1,0:T(8,128)(2,1)S(1)}, u32[]{:S(2)}, u32[]{:S(2)}) collective-permute-start(bf16[8,2,32,128]{3,2,1,0:T(8,128)(2,1)S(1)} %all_to_all.20.block_ref), channel_id=1, source_target_pairs={{0,32},{8,40},{16,48},{24,56},{32,64},{40,72},{48,80},{56,88},{64,... | collective-permute-start | bytes 393224 | tf_op jit(solution)/shard_map/ppermute | solution.py:168
  24.6 5.2 %collective-permute-done.block_ref = bf16[8,2,32,128]{3,2,1,0:T(8,128)(2,1)S(1)} collective-permute-done((bf16[8,2,32,128]{3,2,1,0:T(8,128)(2,1)S(1)}, bf16[8,2,32,128]{3,2,1,0:T(8,128)(2,1)S(1)}, u32[]{:S(2)}, u32[]{:S(2)}) %collective-permute-start) | collective-permute-done | bytes 131104 | tf_op jit(solution)/shard_map/ppermute | solution.py:168
  29.8 0.9 %broadcast_select_fusion = bf16[4,8,2,32,128]{4,3,2,1,0:T(8,128)(2,1)} fusion(pred[4]{0:T(512)(128)(4,1)S(1)} %iota_compare_fusion, bf16[8,2,32,128]{3,2,1,0:T(8,128)(2,1)S(1)} %collective-permute-done.block_ref, bf16[8,2,32,128]{3,2,1,0:T(8,128)(2,1)S(1)} %all_to_all.20.block_ref), kind=kLoop, calls=%fused_computation.1 | loop fusion | flops 262144 | bytes 786436 | tf_op jit(solution)/shard_map/jit(_where)/select_n | solution.py:170
  30.7 4.3 %all-to-all-start.1 = ((bf16[4,8,2,32,128]{4,3,2,1,0:T(8,128)(2,1)}), bf16[4,8,2,32,128]{4,3,2,1,0:T(8,128)(2,1)S(1)}, u32[]{:S(2)}, u32[]{:S(2)}) async-start(bf16[4,8,2,32,128]{4,3,2,1,0:T(8,128)(2,1)} %broadcast_select_fusion), calls=%async_computation.1 | async-start | bytes 1048576 | tf_op jit(solution)/shard_map/all_to_all | solution.py:171
  35.0 4.0 %own.1 = (bf16[256,2048]{1,0:T(8,128)(2,1)S(1)}, f32[8,2,32,128]{3,2,1,0:T(8,128)S(1)}) custom-call(s32[1]{0:T(128)} %bitcast.ctx_ref, bf16[8,2,32,128]{3,2,1,0:T(8,128)(2,1)S(1)} %all_to_all.20.block_ref, bf16[256,2048]{1,0:T(8,128)(2,1)S(1)} %copy-done, bf16[256,2048]{1,0:T(8,128)(2,1)S(1)} %copy-done.1, f32[16,256]{1,0:T(8,128)S(1)} %copy-done.7, ...), custom_call_target="tpu_custom_call" | custom-call | tf_op jit(solution)/shard_map/own/pallas_call | solution.py:109
  39.1 1.0 %copy-done.2 = bf16[256,2048]{1,0:T(8,128)(2,1)} copy-done((bf16[256,2048]{1,0:T(8,128)(2,1)}, bf16[256,2048]{1,0:T(8,128)(2,1)S(1)}, u32[]{:S(2)}) %copy-start.2) | copy-done | bytes 1048600
  40.1 3.0 %all-to-all-done.1.slots_ref = bf16[4,8,2,32,128]{4,3,2,1,0:T(8,128)(2,1)S(1)} async-done(((bf16[4,8,2,32,128]{4,3,2,1,0:T(8,128)(2,1)}), bf16[4,8,2,32,128]{4,3,2,1,0:T(8,128)(2,1)S(1)}, u32[]{:S(2)}, u32[]{:S(2)}) %all-to-all-start.1) | async-done | bytes 524320 | tf_op jit(solution)/shard_map/all_to_all | solution.py:171
  43.1 8.5 %rest.1 = (bf16[256,2048]{1,0:T(8,128)(2,1)S(1)}, bf16[4,8,2,32,128]{4,3,2,1,0:T(8,128)(2,1)}) custom-call(s32[1]{0:T(128)} %bitcast.ctx_ref, bf16[4,8,2,32,128]{4,3,2,1,0:T(8,128)(2,1)S(1)} %all-to-all-done.1.slots_ref, bf16[256,2048]{1,0:T(8,128)(2,1)S(1)} %copy-done, bf16[256,2048]{1,0:T(8,128)(2,1)S(1)} %copy-done.1, f32[16,256]{1,0:T(8,128)S(1)} %copy-done.7, ...), custom_call_target="tpu_custom_call" | custom-call | tf_op jit(solution)/shard_map/rest/pallas_call | solution.py:109
  51.6 1.0 %copy-done.4 = bf16[256,2048]{1,0:T(8,128)(2,1)} copy-done((bf16[256,2048]{1,0:T(8,128)(2,1)}, bf16[256,2048]{1,0:T(8,128)(2,1)S(1)}, u32[]{:S(2)}) %copy-start.4) | copy-done | bytes 1048600
  52.5 3.6 %all-to-all-start.2 = ((bf16[4,8,2,32,128]{4,3,2,1,0:T(8,128)(2,1)}), bf16[4,8,2,32,128]{4,3,2,1,0:T(8,128)(2,1)S(1)}, u32[]{:S(2)}, u32[]{:S(2)}) async-start(bf16[4,8,2,32,128]{4,3,2,1,0:T(8,128)(2,1)} %get-tuple-element.22), calls=%async_computation.2 | async-start | bytes 1048576 | tf_op jit(solution)/shard_map/all_to_all | solution.py:179
  56.2 4.0 %prev.1 = (bf16[256,2048]{1,0:T(8,128)(2,1)S(1)}, f32[8,2,32,128]{3,2,1,0:T(8,128)S(1)}) custom-call(s32[1]{0:T(128)} %bitcast.ctx_ref, bf16[8,2,32,128]{3,2,1,0:T(8,128)(2,1)S(1)} %collective-permute-done.block_ref, bf16[256,2048]{1,0:T(8,128)(2,1)S(1)} %copy-done, bf16[256,2048]{1,0:T(8,128)(2,1)S(1)} %copy-done.1, f32[16,256]{1,0:T(8,128)S(1)} %copy-done.7, ...), custom_call_target="tpu_custom_call" | custom-call | tf_op jit(solution)/shard_map/prev/pallas_call | solution.py:109
  60.3 1.0 %copy-done.6 = bf16[256,2048]{1,0:T(8,128)(2,1)} copy-done((bf16[256,2048]{1,0:T(8,128)(2,1)}, bf16[256,2048]{1,0:T(8,128)(2,1)S(1)}, u32[]{:S(2)}) %copy-start.6) | copy-done | bytes 1048600
  61.2 2.9 %all-to-all-done.2.back_ref = bf16[4,8,2,32,128]{4,3,2,1,0:T(8,128)(2,1)S(1)} async-done(((bf16[4,8,2,32,128]{4,3,2,1,0:T(8,128)(2,1)}), bf16[4,8,2,32,128]{4,3,2,1,0:T(8,128)(2,1)S(1)}, u32[]{:S(2)}, u32[]{:S(2)}) %all-to-all-start.2) | async-done | bytes 524320 | tf_op jit(solution)/shard_map/all_to_all | solution.py:179
  64.1 0.1 prev_sum.1
  64.2 9.8 %collective-permute-start.1 = (bf16[8,2,32,128]{3,2,1,0:T(8,128)(2,1)S(1)}, bf16[8,2,32,128]{3,2,1,0:T(8,128)(2,1)S(1)}, u32[]{:S(2)}, u32[]{:S(2)}) collective-permute-start(bf16[8,2,32,128]{3,2,1,0:T(8,128)(2,1)S(1)} %prev_sum.1), channel_id=1, source_target_pairs={{32,0},{40,8},{48,16},{56,24},{64,32},{72,40},{80,48},{88,56},{96,... | collective-permute-start | bytes 393224 | tf_op jit(solution)/shard_map/ppermute | solution.py:186
  74.0 0.1 own_sum.1.a_ref
  74.2 2.4 %collective-permute-done.1.b_ref = bf16[8,2,32,128]{3,2,1,0:T(8,128)(2,1)S(1)} collective-permute-done((bf16[8,2,32,128]{3,2,1,0:T(8,128)(2,1)S(1)}, bf16[8,2,32,128]{3,2,1,0:T(8,128)(2,1)S(1)}, u32[]{:S(2)}, u32[]{:S(2)}) %collective-permute-start.1) | collective-permute-done | bytes 131104 | tf_op jit(solution)/shard_map/ppermute | solution.py:186
  76.5 0.7 add.16
  77.2 4.9 %all-to-all-start.3 = ((bf16[8,2,32,128]{3,2,1,0:T(8,128)(2,1)}), bf16[8,2,32,128]{3,2,1,0:T(8,128)(2,1)S(1)}, u32[]{:S(2)}, u32[]{:S(2)}) async-start(bf16[8,2,32,128]{3,2,1,0:T(8,128)(2,1)} %add.16), calls=%async_computation.3 | async-start | bytes 262144 | tf_op jit(solution)/shard_map/all_to_all | solution.py:189
  82.1 2.7 %multiply_convert_fusion = bf16[256,2048]{1,0:T(8,128)(2,1)} fusion(bf16[256,2048]{1,0:T(8,128)(2,1)} %copy-done.6, bf16[256,2048]{1,0:T(8,128)(2,1)S(1)} %copy-done.5, bf16[256,2048]{1,0:T(8,128)(2,1)S(1)} %copy-done.3), kind=kLoop, calls=%fused_computation | loop fusion | flops 3670016 | bytes 4194304 | tf_op jit(solution)/shard_map/convert_element_type | solution.py:184
  84.8 4.1 %all-to-all-done.3.pair_ref = bf16[8,2,32,128]{3,2,1,0:T(8,128)(2,1)S(1)} async-done(((bf16[8,2,32,128]{3,2,1,0:T(8,128)(2,1)}), bf16[8,2,32,128]{3,2,1,0:T(8,128)(2,1)S(1)}, u32[]{:S(2)}, u32[]{:S(2)}) %all-to-all-start.3) | async-done | bytes 131104 | tf_op jit(solution)/shard_map/all_to_all | solution.py:189
  88.9 0.7 unpack.1
  (18 shorter events, 0.0 us)
Async XLA Ops:
  2.2 32.8 %copy-start = (bf16[256,2048]{1,0:T(8,128)(2,1)S(1)}, bf16[256,2048]{1,0:T(8,128)(2,1)}, u32[]{:S(2)}) copy-start(bf16[256,2048]{1,0:T(8,128)(2,1)} %q_ref.5) | copy-start | bytes 3145732
  2.2 32.8 %copy-start.1 = (bf16[256,2048]{1,0:T(8,128)(2,1)S(1)}, bf16[256,2048]{1,0:T(8,128)(2,1)}, u32[]{:S(2)}) copy-start(bf16[256,2048]{1,0:T(8,128)(2,1)} %do_ref.5) | copy-start | bytes 3145732
  2.2 32.8 %copy-start.7 = (f32[16,256]{1,0:T(8,128)S(1)}, f32[16,256]{1,0:T(8,128)}, u32[]{:S(2)}) copy-start(f32[16,256]{1,0:T(8,128)} %ln_ref.5) | copy-start | bytes 49156
  2.2 32.8 %copy-start.8 = (f32[16,256]{1,0:T(8,128)S(1)}, f32[16,256]{1,0:T(8,128)}, u32[]{:S(2)}) copy-start(f32[16,256]{1,0:T(8,128)} %dl_ref.5) | copy-start | bytes 49156
  2.2 32.8 %copy-start.9 = (s32[256]{0:T(256)S(1)}, s32[256]{0:T(256)}, u32[]{:S(2)}) copy-start(s32[256]{0:T(256)} %param.13) | copy-start | bytes 3076
  16.4 13.4 %collective-permute-start = (bf16[8,2,32,128]{3,2,1,0:T(8,128)(2,1)S(1)}, bf16[8,2,32,128]{3,2,1,0:T(8,128)(2,1)S(1)}, u32[]{:S(2)}, u32[]{:S(2)}) collective-permute-start(bf16[8,2,32,128]{3,2,1,0:T(8,128)(2,1)S(1)} %all_to_all.20.block_ref), channel_id=1, source_target_pairs={{0,32},{8,40},{16,48},{24,56},{32,64},{40,72},{48,80},{56,88},{64,... | collective-permute-start | bytes 393224 | tf_op jit(solution)/shard_map/ppermute | solution.py:168
  30.7 12.4 %all-to-all-start.1 = ((bf16[4,8,2,32,128]{4,3,2,1,0:T(8,128)(2,1)}), bf16[4,8,2,32,128]{4,3,2,1,0:T(8,128)(2,1)S(1)}, u32[]{:S(2)}, u32[]{:S(2)}) async-start(bf16[4,8,2,32,128]{4,3,2,1,0:T(8,128)(2,1)} %broadcast_select_fusion), calls=%async_computation.1 | async-start | bytes 1048576 | tf_op jit(solution)/shard_map/all_to_all | solution.py:171
  39.1 1.0 %copy-start.2 = (bf16[256,2048]{1,0:T(8,128)(2,1)}, bf16[256,2048]{1,0:T(8,128)(2,1)S(1)}, u32[]{:S(2)}) copy-start(bf16[256,2048]{1,0:T(8,128)(2,1)S(1)} %get-tuple-element.16) | copy-start | bytes 3145732
  51.6 1.0 %copy-start.4 = (bf16[256,2048]{1,0:T(8,128)(2,1)}, bf16[256,2048]{1,0:T(8,128)(2,1)S(1)}, u32[]{:S(2)}) copy-start(bf16[256,2048]{1,0:T(8,128)(2,1)S(1)} %get-tuple-element.18) | copy-start | bytes 3145732
  52.5 11.5 %all-to-all-start.2 = ((bf16[4,8,2,32,128]{4,3,2,1,0:T(8,128)(2,1)}), bf16[4,8,2,32,128]{4,3,2,1,0:T(8,128)(2,1)S(1)}, u32[]{:S(2)}, u32[]{:S(2)}) async-start(bf16[4,8,2,32,128]{4,3,2,1,0:T(8,128)(2,1)} %get-tuple-element.22), calls=%async_computation.2 | async-start | bytes 1048576 | tf_op jit(solution)/shard_map/all_to_all | solution.py:179
  60.2 1.0 %copy-start.6 = (bf16[256,2048]{1,0:T(8,128)(2,1)}, bf16[256,2048]{1,0:T(8,128)(2,1)S(1)}, u32[]{:S(2)}) copy-start(bf16[256,2048]{1,0:T(8,128)(2,1)S(1)} %get-tuple-element.21) | copy-start | bytes 3145732
  64.1 18.0 %copy-start.5 = (bf16[256,2048]{1,0:T(8,128)(2,1)S(1)}, bf16[256,2048]{1,0:T(8,128)(2,1)}, u32[]{:S(2)}) copy-start(bf16[256,2048]{1,0:T(8,128)(2,1)} %copy-done.4) | copy-start | bytes 3145732
  64.2 17.9 %copy-start.3 = (bf16[256,2048]{1,0:T(8,128)(2,1)S(1)}, bf16[256,2048]{1,0:T(8,128)(2,1)}, u32[]{:S(2)}) copy-start(bf16[256,2048]{1,0:T(8,128)(2,1)} %copy-done.2) | copy-start | bytes 3145732
  64.2 12.3 %collective-permute-start.1 = (bf16[8,2,32,128]{3,2,1,0:T(8,128)(2,1)S(1)}, bf16[8,2,32,128]{3,2,1,0:T(8,128)(2,1)S(1)}, u32[]{:S(2)}, u32[]{:S(2)}) collective-permute-start(bf16[8,2,32,128]{3,2,1,0:T(8,128)(2,1)S(1)} %prev_sum.1), channel_id=1, source_target_pairs={{32,0},{40,8},{48,16},{56,24},{64,32},{72,40},{80,48},{88,56},{96,... | collective-permute-start | bytes 393224 | tf_op jit(solution)/shard_map/ppermute | solution.py:186
  77.2 11.6 %all-to-all-start.3 = ((bf16[8,2,32,128]{3,2,1,0:T(8,128)(2,1)}), bf16[8,2,32,128]{3,2,1,0:T(8,128)(2,1)S(1)}, u32[]{:S(2)}, u32[]{:S(2)}) async-start(bf16[8,2,32,128]{3,2,1,0:T(8,128)(2,1)} %add.16), calls=%async_computation.3 | async-start | bytes 262144 | tf_op jit(solution)/shard_map/all_to_all | solution.py:189

commit v3 on v2

--- a/solution.py
+++ b/solution.py
@@ -13,6 +13,8 @@
 GROUP_HEADS = 16
 HEAD_DEVS = 8
 PIECE = ROWS // HEAD_DEVS
+PART = 4
+PARTS = GROUP_HEADS // PART
 ROW_LEN = 4
 SCALE = HD ** (-0.5)
 LOG2E = math.log2(math.e)
@@ -28,10 +30,16 @@
     return ((row - jnp.where(slot > x, 1, 0)) * ROW_LEN + slot) * ROWS
 
 
-def pack_kernel(keys_ref, values_ref, out_ref):
-    for h in range(HEAD_DEVS):
-        out_ref[h, 0] = keys_ref[:, h * HD : (h + 1) * HD]
-        out_ref[h, 1] = values_ref[:, h * HD : (h + 1) * HD]
+def pack_kernel(keys_ref, values_ref, starts_ref, out_ref, first_ref, sem, first_sem):
+    copies = [
+        pltpu.make_async_copy(ref.at[:, pl.ds(h * HD, HD)], out_ref.at[h, i], sem.at[i, h])
+        for i, ref in enumerate((keys_ref, values_ref))
+        for h in range(HEAD_DEVS)
+    ] + [pltpu.make_async_copy(starts_ref, first_ref, first_sem)]
+    for copy in copies:
+        copy.start()
+    for copy in copies:
+        copy.wait()
 
 
 def unpack_kernel(pair_ref, keys_ref, values_ref):
@@ -76,36 +84,88 @@
     ref[:, 1] = acc_ref[1, part].astype(ref.dtype).reshape(HEAD_DEVS, PIECE, HD)
 
 
-def one_kernel(offset, ctx_ref, block_ref, q_ref, do_ref, ln_ref, dl_ref, ds_ref,
-               dq_ref, grads_ref, acc_ref, mask_ref, kv_ref, kt_ref):
+def part_copies(src, dst, sem):
+    cols = [pl.ds(p * PART * HD, PART * HD) for p in range(PARTS)]
+    return [pltpu.make_async_copy(src.at[:, c], dst.at[:, c], sem.at[p]) for p, c in enumerate(cols)]
+
+
+class Sender:
+    def __init__(self, dq_ref, buf, sem):
+        self.buf = buf
+        self.copies = part_copies(buf, dq_ref, sem)
+
+    def __call__(self, col, value):
+        part, head = divmod(col.start // HD, PART)
+        self.buf[:, col] = value.astype(BF16)
+        if head == PART - 1:
+            self.copies[part].start()
+
+    def finish(self):
+        for copy in self.copies:
+            copy.wait()
+
+
+def own_kernel(ctx_ref, own_ref, q_ref, do_ref, ln_ref, dl_ref, ds_ref,
+               dq_ref, grads_ref, acc_ref, mask_ref, kv_ref, kt_ref, buf, sem):
     ctx = ctx_ref[0]
+    emit = Sender(dq_ref, buf, sem)
+    attend(ctx, [(own_ref, ctx * ROWS)], mask_ref, kt_ref, kv_ref, acc_ref, q_ref, do_ref, ln_ref, dl_ref, ds_ref, emit)
+    put_grads(grads_ref, acc_ref, slice(None))
+    emit.finish()
+
+
+def prev_kernel(ctx_ref, prev_ref, q_ref, do_ref, ln_ref, dl_ref, ds_ref, dq_own_ref, dq_rest_ref,
+                dq_ref, grads_ref, acc_ref, mask_ref, kv_ref, kt_ref, buf, sem, total, own_buf, rest_buf, part_sem):
+    ctx = ctx_ref[0]
+    fetches = part_copies(dq_own_ref, own_buf, part_sem.at[0])
+    fetches += part_copies(dq_rest_ref, rest_buf, part_sem.at[1])
+    copies = part_copies(buf, dq_ref, sem)
+    for fetch in fetches:
+        fetch.start()
 
     def emit(col, value):
-        dq_ref[:, col] = value.astype(BF16)
-
-    attend(ctx, [(block_ref, (ctx - offset) * ROWS)], mask_ref, kt_ref, kv_ref, acc_ref, q_ref, do_ref, ln_ref, dl_ref, ds_ref, emit)
+        total[:, col] = value
+        part, head = divmod(col.start // HD, PART)
+        if head < PART - 1 or part < PARTS // 2:
+            return
+        if part == PARTS // 2:
+            for fetch in fetches:
+                fetch.wait()
+        for p in range(part + 1) if part == PARTS // 2 else [part]:
+            cols = slice(p * PART * HD, (p + 1) * PART * HD)
+            value = total[:, cols] + own_buf[:, cols].astype(F32) + rest_buf[:, cols].astype(F32)
+            buf[:, cols] = (value * SCALE).astype(BF16)
+            copies[p].start()
+
+    blocks = [(prev_ref, (ctx - ROW_LEN) * ROWS)]
+    attend(ctx, blocks, mask_ref, kt_ref, kv_ref, acc_ref, q_ref, do_ref, ln_ref, dl_ref, ds_ref, emit)
     put_grads(grads_ref, acc_ref, slice(None))
+    for copy in copies:
+        copy.wait()
 
 
 def rest_kernel(ctx_ref, slots_ref, q_ref, do_ref, ln_ref, dl_ref, ds_ref,
-                dq_ref, grads_ref, acc_ref, mask_ref, kv_ref, kt_ref):
+                dq_ref, grads_ref, acc_ref, mask_ref, kv_ref, kt_ref, buf, sem):
     ctx = ctx_ref[0]
     x = ctx % ROW_LEN
     slots = [(x + 1 + i) % ROW_LEN for i in range(ROW_LEN - 1)]
-
-    def emit(col, value):
-        dq_ref[:, col] = value.astype(BF16)
-
     blocks = [(slots_ref.at[s], slot_base(ctx, s)) for s in slots]
+    emit = Sender(dq_ref, buf, sem)
     attend(ctx, blocks, mask_ref, kt_ref, kv_ref, acc_ref, q_ref, do_ref, ln_ref, dl_ref, ds_ref, emit)
     grads_ref[x] = jnp.zeros((HEAD_DEVS, 2, PIECE, HD), BF16)
     for i, s in enumerate(slots):
         put_grads(grads_ref.at[s], acc_ref, slice(i * ROWS, (i + 1) * ROWS))
-
-
-def vmem_call(kernel, out, *args, name, scratch=()):
-    specs = [pl.BlockSpec(memory_space=pltpu.SMEM if a.size == 1 else pltpu.VMEM) for a in args]
-    outs = jax.tree.map(lambda _: pl.BlockSpec(memory_space=pltpu.VMEM), out)
+    emit.finish()
+
+
+def vmem_call(kernel, out, *args, name, scratch=(), far=(), far_out=()):
+    def space(i, size):
+        return pltpu.HBM if i in far else pltpu.SMEM if size == 1 else pltpu.VMEM
+
+    specs = [pl.BlockSpec(memory_space=space(i, a.size)) for i, a in enumerate(args)]
+    outs = tuple(pl.BlockSpec(memory_space=pltpu.HBM if i in far_out else pltpu.VMEM) for i in range(len(out)))
+    args = [pltpu.with_memory_space_constraint(a, pltpu.HBM) if i in far else a for i, a in enumerate(args)]
+    out = tuple(pltpu.HBM(o.shape, o.dtype) if i in far_out else o for i, o in enumerate(out))
     return pl.pallas_call(
         kernel,
         out_shape=out,
@@ -117,15 +177,20 @@
     )(*args)
 
 
-def attention_call(kernel, count, grads, name, *args):
+def attention_call(kernel, count, outs, name, *args, far=(), scratch=()):
+    wide = (ROWS, GROUP_HEADS * HD)
     scratch = [
         pltpu.VMEM((2, count * ROWS, HD), F32),
         pltpu.VMEM((count * ROWS, ROWS), F32),
         pltpu.VMEM((2, count * ROWS, HD), BF16),
         pltpu.VMEM((HD, count * ROWS), BF16),
+        pltpu.VMEM(wide, BF16),
+        pltpu.SemaphoreType.DMA((PARTS,)),
+        *scratch,
     ]
-    dq = jax.ShapeDtypeStruct((ROWS, GROUP_HEADS * HD), BF16)
-    return vmem_call(kernel, (dq, grads), *args, name=name, scratch=scratch)
+    far_at = range(len(args), len(args) + len(far))
+    outs = (jax.ShapeDtypeStruct(wide, BF16), *outs)
+    return vmem_call(kernel, outs, *args, *far, name=name, scratch=scratch, far=far_at, far_out=(0,))
 
 
 def prev_sum_kernel(ctx_ref, back_ref, near_ref, out_ref):
@@ -152,7 +217,6 @@
     ctx = lax.axis_index("ctx").astype(jnp.int32)
     x = ctx % ROW_LEN
     ctx_arr = ctx.reshape(1)
-    first = doc_start.reshape(1, ROWS)
     block = (HEAD_DEVS, 2, PIECE, HD)
     rows = [[r * ROW_LEN + s for s in range(ROW_LEN)] for r in range(width // ROW_LEN)]
     up = [(i, i + ROW_LEN) for i in range(width - ROW_LEN)]
@@ -161,31 +225,42 @@
     pieces = jax.ShapeDtypeStruct(block, BF16)
     pieces_f32 = jax.ShapeDtypeStruct(block, F32)
     slots_type = jax.ShapeDtypeStruct((ROW_LEN, *block), BF16)
+    packed, first = vmem_call(
+        pack_kernel,
+        (pieces, jax.ShapeDtypeStruct((1, ROWS), jnp.int32)),
+        keys,
+        values,
+        doc_start.reshape(1, ROWS),
+        name="pack",
+        scratch=(pltpu.SemaphoreType.DMA((2, HEAD_DEVS)), pltpu.SemaphoreType.DMA(())),
+        far=(0, 1, 2),
+    )
     side = (queries, out_grad, log_norm, delta_rows, first)
-
-    packed = pl.pallas_call(pack_kernel, out_shape=pieces, name="pack")(keys, values)
     own = lax.all_to_all(packed, "head", split_axis=0, concat_axis=0, tiled=True)
     prev = lax.ppermute(own, "ctx", up)
     slot = lax.broadcasted_iota(jnp.int32, (ROW_LEN, 1, 1, 1, 1), 0)
     outgoing = jnp.where(slot > x, own[None], prev[None])
     slots = lax.all_to_all(outgoing, "ctx", split_axis=0, concat_axis=0, tiled=True, axis_index_groups=rows)
-    dq_own, own_grads = attention_call(
-        functools.partial(one_kernel, 0), 1, pieces_f32, "own", ctx_arr, own, *side
-    )
+    dq_own, own_grads = attention_call(own_kernel, 1, (pieces_f32,), "own", ctx_arr, own, *side)
     slots, dq_own = lax.optimization_barrier((slots, dq_own))
-    dq_rest, rest = attention_call(rest_kernel, 3, slots_type, "rest", ctx_arr, slots, *side)
+    dq_rest, rest = attention_call(rest_kernel, 3, (slots_type,), "rest", ctx_arr, slots, *side)
 
     rest, prev = lax.optimization_barrier((rest, prev))
     back = lax.all_to_all(rest, "ctx", split_axis=0, concat_axis=0, tiled=True, axis_index_groups=rows)
-    dq_prev, prev_grads = attention_call(
-        functools.partial(one_kernel, ROW_LEN), 1, pieces_f32, "prev", ctx_arr, prev, *side
+    wide = (ROWS, GROUP_HEADS * HD)
+    query_grad, prev_grads = attention_call(
+        prev_kernel, 1, (pieces_f32,), "prev", ctx_arr, prev, *side, far=(dq_own, dq_rest),
+        scratch=(
+            pltpu.VMEM(wide, F32),
+            pltpu.VMEM(wide, BF16),
+            pltpu.VMEM(wide, BF16),
+            pltpu.SemaphoreType.DMA((2, PARTS)),
+        ),
     )
-    query_grad = (dq_own.astype(F32) + dq_rest.astype(F32) + dq_prev.astype(F32)) * SCALE
-    query_grad = query_grad.astype(BF16)
-    prev_sum = vmem_call(prev_sum_kernel, pieces, ctx_arr, back, prev_grads, name="prev_sum")
+    (prev_sum,) = vmem_call(prev_sum_kernel, (pieces,), ctx_arr, back, prev_grads, name="prev_sum")
     from_next = lax.ppermute(prev_sum, "ctx", down)
-    own_sum = vmem_call(own_sum_kernel, pieces_f32, ctx_arr, back, own_grads, name="own_sum")
-    total = vmem_call(add_kernel, pieces, own_sum, from_next, name="add")
+    (own_sum,) = vmem_call(own_sum_kernel, (pieces_f32,), ctx_arr, back, own_grads, name="own_sum")
+    (total,) = vmem_call(add_kernel, (pieces,), own_sum, from_next, name="add")
     returned = lax.all_to_all(total, "head", split_axis=0, concat_axis=0, tiled=True)
     tokens = jax.ShapeDtypeStruct((PIECE, HEAD_DEVS * HD), BF16)
     key_grad, value_grad = vmem_call(unpack_kernel, (tokens, tokens), returned, name="unpack")

time: 90.1 us -> 88.3 us (0.980)
  blocking collectives: 14.2 us -> 25.4 us
  starting transfers between devices: 30.8 us -> 26 us
  waiting for transfers between devices: 17.5 us -> 13.1 us
  local copies, waits for them, and re-layouts: 2.95 us -> 0.02 us
  other arithmetic: 3.62 us -> 0.9 us
  Pallas kernels: 19.7 us -> 21.7 us
    all_to_all x0 -> x1, blocking collectives: none -> 11.4 us  [local(): lax.all_to_all(total, 'head', split_axis=0, concat_axis=0, tiled=True)]
    all_to_all x1 -> x0, starting transfers between devices: 4.85 us -> none  [local(): lax.all_to_all(total, 'head', split_axis=0, concat_axis=0, tiled=True)]
    all_to_all x1 -> x0, waiting for transfers between devices: 4.05 us -> none  [local(): lax.all_to_all(total, 'head', split_axis=0, concat_axis=0, tiled=True)]
    pallas_call x7 -> x8, Pallas kernels: 18.1 us -> 21.7 us  [vmem_call(): pl.pallas_call(kernel, out_shape=out, in_specs=specs, out_specs=outs, scr...]
    unnamed x20 -> x8, local copies, waits for them, and re-layouts: 2.95 us -> 0.02 us
    convert_element_type x1 -> x0, other arithmetic: 2.71 us -> none  [local(): query_grad = query_grad.astype(BF16)]
    pallas_call x1 -> x0, Pallas kernels: 1.55 us -> none  [local(): pl.pallas_call(pack_kernel, out_shape=pieces, name='pack')(keys, values)]
  transfers between devices with their start and end apart: 5 -> 4, of which waited for: 5 -> 4; matrix products, arithmetic and copies ran while one was open for 3% -> 0% of each run, Pallas kernels for 9% -> 12%
where the time goes in v3:
time: 88.3 us; the launch traced here: 87.9 us
  starting transfers between devices  26 us (29%)
  blocking collectives  25.4 us (29%)
  Pallas kernels  21.7 us (25%)
  waiting for transfers between devices  13.1 us (15%)
  other arithmetic  0.9 us (1%)
    pallas_call x8, Pallas kernels, vmem_call(): pl.pallas_call(kernel, out_shape=out, in_specs=specs, out_specs=outs, scr...  21.7 us
    all_to_all x1, blocking collectives, local(): lax.all_to_all(packed, 'head', split_axis=0, concat_axis=0, tiled=True)  14 us
    all_to_all x1, blocking collectives, local(): lax.all_to_all(total, 'head', split_axis=0, concat_axis=0, tiled=True)  11.4 us
    ppermute x1, starting transfers between devices, local(): from_next = lax.ppermute(prev_sum, 'ctx', down)  9.71 us
    ppermute x1, starting transfers between devices, local(): prev = lax.ppermute(own, 'ctx', up)  8.21 us
    ppermute x1, waiting for transfers between devices, local(): prev = lax.ppermute(own, 'ctx', up)  5.17 us
    all_to_all x1, starting transfers between devices, local(): lax.all_to_all(outgoing, 'ctx', split_axis=0, concat_axis=0, tiled=True,...  4.42 us
    all_to_all x1, starting transfers between devices, local(): lax.all_to_all(rest, 'ctx', split_axis=0, concat_axis=0, tiled=True, axis...  3.66 us
  transfers between devices with their start and end apart: 4, of which 4 were waited for; matrix products, arithmetic and copies ran while one was open for 0% of the time, Pallas kernels for 12%

profile of v3, /device:TPU:40, one launch (start us, length us, event | category | flops | bytes accessed | tf_op | source)
XLA Modules:
  0.0 87.9 jit_solution(12191997325813730494)
XLA Ops:
  0.6 1.0 %pack.1 = (bf16[8,2,32,128]{3,2,1,0:T(8,128)(2,1)S(1)}, s32[1,256]{1,0:T(1,128)S(1)}) custom-call(bf16[32,1024]{1,0:T(8,128)(2,1)} %keys_ref.1, bf16[32,1024]{1,0:T(8,128)(2,1)} %values_ref.1, s32[1,256]{1,0:T(1,128)} %bitcast.2), custom_call_target="tpu_custom_call" | custom-call | tf_op jit(solution)/shard_map/pack/pallas_call | solution.py:169
  1.7 0.0 copy-start
  1.7 0.0 copy-start.1
  1.7 14.0 %all_to_all.20.own_ref = bf16[8,2,32,128]{3,2,1,0:T(8,128)(2,1)S(1)} all-to-all(bf16[8,2,32,128]{3,2,1,0:T(8,128)(2,1)S(1)} %get-tuple-element.17), channel_id=1, replica_groups=mesh['ctx'=64,'head'=8] {'head'}, dimensions={0} | all-to-all | bytes 262144 | tf_op jit(solution)/shard_map/all_to_all | solution.py:239
  15.7 8.2 %collective-permute-start = (bf16[8,2,32,128]{3,2,1,0:T(8,128)(2,1)S(1)}, bf16[8,2,32,128]{3,2,1,0:T(8,128)(2,1)S(1)}, u32[]{:S(2)}, u32[]{:S(2)}) collective-permute-start(bf16[8,2,32,128]{3,2,1,0:T(8,128)(2,1)S(1)} %all_to_all.20.own_ref), channel_id=1, source_target_pairs={{0,32},{8,40},{16,48},{24,56},{32,64},{40,72},{48,80},{56,88},{64,... | collective-permute-start | bytes 393224 | tf_op jit(solution)/shard_map/ppermute | solution.py:240
  23.9 5.2 %collective-permute-done.prev_ref = bf16[8,2,32,128]{3,2,1,0:T(8,128)(2,1)S(1)} collective-permute-done((bf16[8,2,32,128]{3,2,1,0:T(8,128)(2,1)S(1)}, bf16[8,2,32,128]{3,2,1,0:T(8,128)(2,1)S(1)}, u32[]{:S(2)}, u32[]{:S(2)}) %collective-permute-start) | collective-permute-done | bytes 131104 | tf_op jit(solution)/shard_map/ppermute | solution.py:240
  29.1 0.9 %broadcast_select_fusion = bf16[4,8,2,32,128]{4,3,2,1,0:T(8,128)(2,1)} fusion(pred[4]{0:T(512)(128)(4,1)S(1)} %iota_compare_fusion, bf16[8,2,32,128]{3,2,1,0:T(8,128)(2,1)S(1)} %collective-permute-done.prev_ref, bf16[8,2,32,128]{3,2,1,0:T(8,128)(2,1)S(1)} %all_to_all.20.own_ref), kind=kLoop, calls=%fused_computation | loop fusion | flops 262144 | bytes 786436 | tf_op jit(solution)/shard_map/jit(_where)/select_n | solution.py:242
  30.0 4.4 %all-to-all-start.1 = ((bf16[4,8,2,32,128]{4,3,2,1,0:T(8,128)(2,1)}), bf16[4,8,2,32,128]{4,3,2,1,0:T(8,128)(2,1)S(1)}, u32[]{:S(2)}, u32[]{:S(2)}) async-start(bf16[4,8,2,32,128]{4,3,2,1,0:T(8,128)(2,1)} %broadcast_select_fusion), calls=%async_computation.1 | async-start | bytes 1048576 | tf_op jit(solution)/shard_map/all_to_all | solution.py:243
  34.4 0.0 copy-done
  34.4 0.0 copy-done.1
  34.4 0.0 copy-done.2
  34.4 0.0 copy-done.3
  34.4 4.9 %own.1 = (bf16[256,2048]{1,0:T(8,128)(2,1)}, f32[8,2,32,128]{3,2,1,0:T(8,128)S(1)}) custom-call(s32[1]{0:T(128)} %bitcast.ctx_ref, bf16[8,2,32,128]{3,2,1,0:T(8,128)(2,1)S(1)} %all_to_all.20.own_ref, bf16[256,2048]{1,0:T(8,128)(2,1)S(1)} %copy-done, bf16[256,2048]{1,0:T(8,128)(2,1)S(1)} %copy-done.1, f32[16,256]{1,0:T(8,128)S(1)} %copy-done.2, ...), custom_call_target="tpu_custom_call" | custom-call | tf_op jit(solution)/shard_map/own/pallas_call | solution.py:169
  39.3 3.2 %all-to-all-done.1.slots_ref = bf16[4,8,2,32,128]{4,3,2,1,0:T(8,128)(2,1)S(1)} async-done(((bf16[4,8,2,32,128]{4,3,2,1,0:T(8,128)(2,1)}), bf16[4,8,2,32,128]{4,3,2,1,0:T(8,128)(2,1)S(1)}, u32[]{:S(2)}, u32[]{:S(2)}) %all-to-all-start.1) | async-done | bytes 524320 | tf_op jit(solution)/shard_map/all_to_all | solution.py:243
  42.5 9.4 %rest.1 = (bf16[256,2048]{1,0:T(8,128)(2,1)}, bf16[4,8,2,32,128]{4,3,2,1,0:T(8,128)(2,1)}) custom-call(s32[1]{0:T(128)} %bitcast.ctx_ref, bf16[4,8,2,32,128]{4,3,2,1,0:T(8,128)(2,1)S(1)} %all-to-all-done.1.slots_ref, bf16[256,2048]{1,0:T(8,128)(2,1)S(1)} %copy-done, bf16[256,2048]{1,0:T(8,128)(2,1)S(1)} %copy-done.1, f32[16,256]{1,0:T(8,128)S(1)} %copy-done.2, ...), custom_call_target="tpu_custom_call" | custom-call | tf_op jit(solution)/shard_map/rest/pallas_call | solution.py:169
  51.9 3.7 %all-to-all-start.2 = ((bf16[4,8,2,32,128]{4,3,2,1,0:T(8,128)(2,1)}), bf16[4,8,2,32,128]{4,3,2,1,0:T(8,128)(2,1)S(1)}, u32[]{:S(2)}, u32[]{:S(2)}) async-start(bf16[4,8,2,32,128]{4,3,2,1,0:T(8,128)(2,1)} %get-tuple-element.26), calls=%async_computation.2 | async-start | bytes 1048576 | tf_op jit(solution)/shard_map/all_to_all | solution.py:249
  55.6 5.5 %prev.1 = (bf16[256,2048]{1,0:T(8,128)(2,1)}, f32[8,2,32,128]{3,2,1,0:T(8,128)S(1)}) custom-call(s32[1]{0:T(128)} %bitcast.ctx_ref, bf16[8,2,32,128]{3,2,1,0:T(8,128)(2,1)S(1)} %collective-permute-done.prev_ref, bf16[256,2048]{1,0:T(8,128)(2,1)S(1)} %copy-done, bf16[256,2048]{1,0:T(8,128)(2,1)S(1)} %copy-done.1, f32[16,256]{1,0:T(8,128)S(1)} %copy-done.2, ...), custom_call_target="tpu_custom_call" | custom-call | tf_op jit(solution)/shard_map/prev/pallas_call | solution.py:169
  61.1 2.3 %all-to-all-done.2.back_ref = bf16[4,8,2,32,128]{4,3,2,1,0:T(8,128)(2,1)S(1)} async-done(((bf16[4,8,2,32,128]{4,3,2,1,0:T(8,128)(2,1)}), bf16[4,8,2,32,128]{4,3,2,1,0:T(8,128)(2,1)S(1)}, u32[]{:S(2)}, u32[]{:S(2)}) %all-to-all-start.2) | async-done | bytes 524320 | tf_op jit(solution)/shard_map/all_to_all | solution.py:249
  63.4 0.1 prev_sum.1
  63.5 9.7 %collective-permute-start.1 = (bf16[8,2,32,128]{3,2,1,0:T(8,128)(2,1)S(1)}, bf16[8,2,32,128]{3,2,1,0:T(8,128)(2,1)S(1)}, u32[]{:S(2)}, u32[]{:S(2)}) collective-permute-start(bf16[8,2,32,128]{3,2,1,0:T(8,128)(2,1)S(1)} %prev_sum.1), channel_id=1, source_target_pairs={{32,0},{40,8},{48,16},{56,24},{64,32},{72,40},{80,48},{88,56},{96,... | collective-permute-start | bytes 393224 | tf_op jit(solution)/shard_map/ppermute | solution.py:261
  73.3 0.1 own_sum.1.a_ref
  73.4 2.4 %collective-permute-done.1.b_ref = bf16[8,2,32,128]{3,2,1,0:T(8,128)(2,1)S(1)} collective-permute-done((bf16[8,2,32,128]{3,2,1,0:T(8,128)(2,1)S(1)}, bf16[8,2,32,128]{3,2,1,0:T(8,128)(2,1)S(1)}, u32[]{:S(2)}, u32[]{:S(2)}) %collective-permute-start.1) | collective-permute-done | bytes 131104 | tf_op jit(solution)/shard_map/ppermute | solution.py:261
  75.8 11.4 %all_to_all.21.pair_ref = bf16[8,2,32,128]{3,2,1,0:T(8,128)(2,1)S(1)} all-to-all(bf16[8,2,32,128]{3,2,1,0:T(8,128)(2,1)S(1)} %add.6), channel_id=1, replica_groups=mesh['ctx'=64,'head'=8] {'head'}, dimensions={0} | all-to-all | bytes 262144 | tf_op jit(solution)/shard_map/all_to_all | solution.py:264
  87.2 0.7 unpack.1
  (4 shorter events, 0.0 us)
Async XLA Ops:
  1.7 32.7 %copy-start = (bf16[256,2048]{1,0:T(8,128)(2,1)S(1)}, bf16[256,2048]{1,0:T(8,128)(2,1)}, u32[]{:S(2)}) copy-start(bf16[256,2048]{1,0:T(8,128)(2,1)} %q_ref.5) | copy-start | bytes 3145732
  1.7 32.7 %copy-start.1 = (bf16[256,2048]{1,0:T(8,128)(2,1)S(1)}, bf16[256,2048]{1,0:T(8,128)(2,1)}, u32[]{:S(2)}) copy-start(bf16[256,2048]{1,0:T(8,128)(2,1)} %do_ref.5) | copy-start | bytes 3145732
  15.7 13.4 %collective-permute-start = (bf16[8,2,32,128]{3,2,1,0:T(8,128)(2,1)S(1)}, bf16[8,2,32,128]{3,2,1,0:T(8,128)(2,1)S(1)}, u32[]{:S(2)}, u32[]{:S(2)}) collective-permute-start(bf16[8,2,32,128]{3,2,1,0:T(8,128)(2,1)S(1)} %all_to_all.20.own_ref), channel_id=1, source_target_pairs={{0,32},{8,40},{16,48},{24,56},{32,64},{40,72},{48,80},{56,88},{64,... | collective-permute-start | bytes 393224 | tf_op jit(solution)/shard_map/ppermute | solution.py:240
  30.0 4.4 %copy-start.2 = (f32[16,256]{1,0:T(8,128)S(1)}, f32[16,256]{1,0:T(8,128)}, u32[]{:S(2)}) copy-start(f32[16,256]{1,0:T(8,128)} %ln_ref.5) | copy-start | bytes 49156
  30.0 4.4 %copy-start.3 = (f32[16,256]{1,0:T(8,128)S(1)}, f32[16,256]{1,0:T(8,128)}, u32[]{:S(2)}) copy-start(f32[16,256]{1,0:T(8,128)} %dl_ref.5) | copy-start | bytes 49156
  30.0 12.5 %all-to-all-start.1 = ((bf16[4,8,2,32,128]{4,3,2,1,0:T(8,128)(2,1)}), bf16[4,8,2,32,128]{4,3,2,1,0:T(8,128)(2,1)S(1)}, u32[]{:S(2)}, u32[]{:S(2)}) async-start(bf16[4,8,2,32,128]{4,3,2,1,0:T(8,128)(2,1)} %broadcast_select_fusion), calls=%async_computation.1 | async-start | bytes 1048576 | tf_op jit(solution)/shard_map/all_to_all | solution.py:243
  51.9 11.5 %all-to-all-start.2 = ((bf16[4,8,2,32,128]{4,3,2,1,0:T(8,128)(2,1)}), bf16[4,8,2,32,128]{4,3,2,1,0:T(8,128)(2,1)S(1)}, u32[]{:S(2)}, u32[]{:S(2)}) async-start(bf16[4,8,2,32,128]{4,3,2,1,0:T(8,128)(2,1)} %get-tuple-element.26), calls=%async_computation.2 | async-start | bytes 1048576 | tf_op jit(solution)/shard_map/all_to_all | solution.py:249
  63.5 12.2 %collective-permute-start.1 = (bf16[8,2,32,128]{3,2,1,0:T(8,128)(2,1)S(1)}, bf16[8,2,32,128]{3,2,1,0:T(8,128)(2,1)S(1)}, u32[]{:S(2)}, u32[]{:S(2)}) collective-permute-start(bf16[8,2,32,128]{3,2,1,0:T(8,128)(2,1)S(1)} %prev_sum.1), channel_id=1, source_target_pairs={{32,0},{40,8},{48,16},{56,24},{64,32},{72,40},{80,48},{88,56},{96,... | collective-permute-start | bytes 393224 | tf_op jit(solution)/shard_map/ppermute | solution.py:261

commit v4 on v3

--- a/solution.py
+++ b/solution.py
@@ -42,10 +42,29 @@
         copy.wait()
 
 
-def unpack_kernel(pair_ref, keys_ref, values_ref):
-    for h in range(HEAD_DEVS):
-        keys_ref[:, h * HD : (h + 1) * HD] = pair_ref[h, 0]
-        values_ref[:, h * HD : (h + 1) * HD] = pair_ref[h, 1]
+def unpack_kernel(pair_ref, keys_ref, values_ref, sem):
+    copies = [
+        pltpu.make_async_copy(pair_ref.at[h, i], ref.at[:, pl.ds(h * HD, HD)], sem.at[i, h])
+        for i, ref in enumerate((keys_ref, values_ref))
+        for h in range(HEAD_DEVS)
+    ]
+    for copy in copies:
+        copy.start()
+    for copy in copies:
+        copy.wait()
+
+
+def fill_kernel(ctx_ref, own_ref, prev_ref, out_ref, sem):
+    x = ctx_ref[0] % ROW_LEN
+    for s in range(ROW_LEN):
+        for ref, ours in ((own_ref, s > x), (prev_ref, s <= x)):
+
+            @pl.when(ours)
+            def _(ref=ref):
+                pltpu.make_async_copy(ref, out_ref.at[s], sem.at[s]).start()
+
+    for s in range(ROW_LEN):
+        pltpu.make_async_copy(own_ref, out_ref.at[s], sem.at[s]).wait()
 
 
 def attend(ctx, blocks, mask_ref, kt_ref, kv_ref, acc_ref, q_ref, do_ref, ln_ref, dl_ref, ds_ref, emit):
@@ -215,7 +234,6 @@
 
 def local(width, queries, keys, values, out_grad, log_norm, delta_rows, doc_start):
     ctx = lax.axis_index("ctx").astype(jnp.int32)
-    x = ctx % ROW_LEN
     ctx_arr = ctx.reshape(1)
     block = (HEAD_DEVS, 2, PIECE, HD)
     rows = [[r * ROW_LEN + s for s in range(ROW_LEN)] for r in range(width // ROW_LEN)]
@@ -238,8 +256,10 @@
     side = (queries, out_grad, log_norm, delta_rows, first)
     own = lax.all_to_all(packed, "head", split_axis=0, concat_axis=0, tiled=True)
     prev = lax.ppermute(own, "ctx", up)
-    slot = lax.broadcasted_iota(jnp.int32, (ROW_LEN, 1, 1, 1, 1), 0)
-    outgoing = jnp.where(slot > x, own[None], prev[None])
+    (outgoing,) = vmem_call(
+        fill_kernel, (slots_type,), ctx_arr, own, prev, name="fill",
+        scratch=(pltpu.SemaphoreType.DMA((ROW_LEN,)),), far_out=(0,),
+    )
     slots = lax.all_to_all(outgoing, "ctx", split_axis=0, concat_axis=0, tiled=True, axis_index_groups=rows)
     dq_own, own_grads = attention_call(own_kernel, 1, (pieces_f32,), "own", ctx_arr, own, *side)
     slots, dq_own = lax.optimization_barrier((slots, dq_own))
@@ -263,7 +283,10 @@
     (total,) = vmem_call(add_kernel, (pieces,), own_sum, from_next, name="add")
     returned = lax.all_to_all(total, "head", split_axis=0, concat_axis=0, tiled=True)
     tokens = jax.ShapeDtypeStruct((PIECE, HEAD_DEVS * HD), BF16)
-    key_grad, value_grad = vmem_call(unpack_kernel, (tokens, tokens), returned, name="unpack")
+    key_grad, value_grad = vmem_call(
+        unpack_kernel, (tokens, tokens), returned, name="unpack",
+        scratch=(pltpu.SemaphoreType.DMA((2, HEAD_DEVS)),), far_out=(0, 1),
+    )
     return query_grad, key_grad, value_grad
 
 

time: 88.3 us -> 88.4 us (level)
  Pallas kernels: 21.7 us -> 22.9 us
  other arithmetic: 0.9 us -> 0 us
    pallas_call x8 -> x9, Pallas kernels: 21.7 us -> 22.9 us  [vmem_call(): pl.pallas_call(kernel, out_shape=out, in_specs=specs, out_specs=outs, scr...]
    select_n x1 -> x0, other arithmetic: 0.9 us -> none  [local(): outgoing = jnp.where(slot > x, own[None], prev[None])]
where the time goes in v4:
time: 88.4 us; the launch traced here: 88 us
  starting transfers between devices  25.9 us (29%)
  blocking collectives  25.4 us (29%)
  Pallas kernels  22.9 us (26%)
  waiting for transfers between devices  12.9 us (15%)
  between operations  0.92 us (1%)
    pallas_call x9, Pallas kernels, vmem_call(): pl.pallas_call(kernel, out_shape=out, in_specs=specs, out_specs=outs, scr...  22.9 us
    all_to_all x1, blocking collectives, local(): lax.all_to_all(packed, 'head', split_axis=0, concat_axis=0, tiled=True)  14 us
    all_to_all x1, blocking collectives, local(): lax.all_to_all(total, 'head', split_axis=0, concat_axis=0, tiled=True)  11.4 us
    ppermute x1, starting transfers between devices, local(): from_next = lax.ppermute(prev_sum, 'ctx', down)  9.71 us
    ppermute x1, starting transfers between devices, local(): prev = lax.ppermute(own, 'ctx', up)  8.21 us
    ppermute x1, waiting for transfers between devices, local(): prev = lax.ppermute(own, 'ctx', up)  5.19 us
    all_to_all x1, starting transfers between devices, local(): lax.all_to_all(outgoing, 'ctx', split_axis=0, concat_axis=0, tiled=True,...  4.3 us
    all_to_all x1, starting transfers between devices, local(): lax.all_to_all(rest, 'ctx', split_axis=0, concat_axis=0, tiled=True, axis...  3.66 us
  transfers between devices with their start and end apart: 4, of which 4 were waited for; matrix products, arithmetic and copies ran while one was open for 0% of the time, Pallas kernels for 12%

profile of v4, /device:TPU:40, one launch (start us, length us, event | category | flops | bytes accessed | tf_op | source)
XLA Modules:
  0.0 88.0 jit_solution(4889572640916873734)
XLA Ops:
  0.6 0.0 copy-start.2
  0.6 0.0 copy-start.3
  0.7 1.0 %pack.1 = (bf16[8,2,32,128]{3,2,1,0:T(8,128)(2,1)S(1)}, s32[1,256]{1,0:T(1,128)S(1)}) custom-call(bf16[32,1024]{1,0:T(8,128)(2,1)} %keys_ref.1, bf16[32,1024]{1,0:T(8,128)(2,1)} %values_ref.1, s32[1,256]{1,0:T(1,128)} %bitcast.2), custom_call_target="tpu_custom_call" | custom-call | tf_op jit(solution)/shard_map/pack/pallas_call | solution.py:188
  1.7 0.0 copy-start
  1.7 0.0 copy-start.1
  1.7 14.0 %all_to_all.20.own_ref = bf16[8,2,32,128]{3,2,1,0:T(8,128)(2,1)S(1)} all-to-all(bf16[8,2,32,128]{3,2,1,0:T(8,128)(2,1)S(1)} %get-tuple-element.17), channel_id=1, replica_groups=mesh['ctx'=64,'head'=8] {'head'}, dimensions={0} | all-to-all | bytes 262144 | tf_op jit(solution)/shard_map/all_to_all | solution.py:257
  15.7 8.2 %collective-permute-start = (bf16[8,2,32,128]{3,2,1,0:T(8,128)(2,1)S(1)}, bf16[8,2,32,128]{3,2,1,0:T(8,128)(2,1)S(1)}, u32[]{:S(2)}, u32[]{:S(2)}) collective-permute-start(bf16[8,2,32,128]{3,2,1,0:T(8,128)(2,1)S(1)} %all_to_all.20.own_ref), channel_id=1, source_target_pairs={{0,32},{8,40},{16,48},{24,56},{32,64},{40,72},{48,80},{56,88},{64,... | collective-permute-start | bytes 393224 | tf_op jit(solution)/shard_map/ppermute | solution.py:258
  23.9 5.2 %collective-permute-done.prev_ref = bf16[8,2,32,128]{3,2,1,0:T(8,128)(2,1)S(1)} collective-permute-done((bf16[8,2,32,128]{3,2,1,0:T(8,128)(2,1)S(1)}, bf16[8,2,32,128]{3,2,1,0:T(8,128)(2,1)S(1)}, u32[]{:S(2)}, u32[]{:S(2)}) %collective-permute-start) | collective-permute-done | bytes 131104 | tf_op jit(solution)/shard_map/ppermute | solution.py:258
  29.1 0.8 fill.1
  29.9 4.3 %all-to-all-start.1 = ((bf16[4,8,2,32,128]{4,3,2,1,0:T(8,128)(2,1)}), bf16[4,8,2,32,128]{4,3,2,1,0:T(8,128)(2,1)S(1)}, u32[]{:S(2)}, u32[]{:S(2)}) async-start(bf16[4,8,2,32,128]{4,3,2,1,0:T(8,128)(2,1)} %fill.1), calls=%async_computation.1 | async-start | bytes 1048576 | tf_op jit(solution)/shard_map/all_to_all | solution.py:263
  34.2 0.0 copy-done
  34.2 0.0 copy-done.1
  34.2 4.9 %own.1 = (bf16[256,2048]{1,0:T(8,128)(2,1)}, f32[8,2,32,128]{3,2,1,0:T(8,128)S(1)}) custom-call(s32[1]{0:T(128)} %bitcast.ctx_ref, bf16[8,2,32,128]{3,2,1,0:T(8,128)(2,1)S(1)} %all_to_all.20.own_ref, bf16[256,2048]{1,0:T(8,128)(2,1)S(1)} %copy-done, bf16[256,2048]{1,0:T(8,128)(2,1)S(1)} %copy-done.1, f32[16,256]{1,0:T(8,128)S(1)} %copy-done.2, ...), custom_call_target="tpu_custom_call" | custom-call | tf_op jit(solution)/shard_map/own/pallas_call | solution.py:188
  39.2 3.1 %all-to-all-done.1.slots_ref = bf16[4,8,2,32,128]{4,3,2,1,0:T(8,128)(2,1)S(1)} async-done(((bf16[4,8,2,32,128]{4,3,2,1,0:T(8,128)(2,1)}), bf16[4,8,2,32,128]{4,3,2,1,0:T(8,128)(2,1)S(1)}, u32[]{:S(2)}, u32[]{:S(2)}) %all-to-all-start.1) | async-done | bytes 524320 | tf_op jit(solution)/shard_map/all_to_all | solution.py:263
  42.3 9.5 %rest.1 = (bf16[256,2048]{1,0:T(8,128)(2,1)}, bf16[4,8,2,32,128]{4,3,2,1,0:T(8,128)(2,1)}) custom-call(s32[1]{0:T(128)} %bitcast.ctx_ref, bf16[4,8,2,32,128]{4,3,2,1,0:T(8,128)(2,1)S(1)} %all-to-all-done.1.slots_ref, bf16[256,2048]{1,0:T(8,128)(2,1)S(1)} %copy-done, bf16[256,2048]{1,0:T(8,128)(2,1)S(1)} %copy-done.1, f32[16,256]{1,0:T(8,128)S(1)} %copy-done.2, ...), custom_call_target="tpu_custom_call" | custom-call | tf_op jit(solution)/shard_map/rest/pallas_call | solution.py:188
  51.8 3.7 %all-to-all-start.2 = ((bf16[4,8,2,32,128]{4,3,2,1,0:T(8,128)(2,1)}), bf16[4,8,2,32,128]{4,3,2,1,0:T(8,128)(2,1)S(1)}, u32[]{:S(2)}, u32[]{:S(2)}) async-start(bf16[4,8,2,32,128]{4,3,2,1,0:T(8,128)(2,1)} %get-tuple-element.26), calls=%async_computation.2 | async-start | bytes 1048576 | tf_op jit(solution)/shard_map/all_to_all | solution.py:269
  55.4 5.6 %prev.1 = (bf16[256,2048]{1,0:T(8,128)(2,1)}, f32[8,2,32,128]{3,2,1,0:T(8,128)S(1)}) custom-call(s32[1]{0:T(128)} %bitcast.ctx_ref, bf16[8,2,32,128]{3,2,1,0:T(8,128)(2,1)S(1)} %collective-permute-done.prev_ref, bf16[256,2048]{1,0:T(8,128)(2,1)S(1)} %copy-done, bf16[256,2048]{1,0:T(8,128)(2,1)S(1)} %copy-done.1, f32[16,256]{1,0:T(8,128)S(1)} %copy-done.2, ...), custom_call_target="tpu_custom_call" | custom-call | tf_op jit(solution)/shard_map/prev/pallas_call | solution.py:188
  61.0 2.3 %all-to-all-done.2.back_ref = bf16[4,8,2,32,128]{4,3,2,1,0:T(8,128)(2,1)S(1)} async-done(((bf16[4,8,2,32,128]{4,3,2,1,0:T(8,128)(2,1)}), bf16[4,8,2,32,128]{4,3,2,1,0:T(8,128)(2,1)S(1)}, u32[]{:S(2)}, u32[]{:S(2)}) %all-to-all-start.2) | async-done | bytes 524320 | tf_op jit(solution)/shard_map/all_to_all | solution.py:269
  63.3 0.1 prev_sum.1
  63.4 9.7 %collective-permute-start.1 = (bf16[8,2,32,128]{3,2,1,0:T(8,128)(2,1)S(1)}, bf16[8,2,32,128]{3,2,1,0:T(8,128)(2,1)S(1)}, u32[]{:S(2)}, u32[]{:S(2)}) collective-permute-start(bf16[8,2,32,128]{3,2,1,0:T(8,128)(2,1)S(1)} %prev_sum.1), channel_id=1, source_target_pairs={{32,0},{40,8},{48,16},{56,24},{64,32},{72,40},{80,48},{88,56},{96,... | collective-permute-start | bytes 393224 | tf_op jit(solution)/shard_map/ppermute | solution.py:281
  73.1 0.1 own_sum.1.a_ref
  73.3 2.4 %collective-permute-done.1.b_ref = bf16[8,2,32,128]{3,2,1,0:T(8,128)(2,1)S(1)} collective-permute-done((bf16[8,2,32,128]{3,2,1,0:T(8,128)(2,1)S(1)}, bf16[8,2,32,128]{3,2,1,0:T(8,128)(2,1)S(1)}, u32[]{:S(2)}, u32[]{:S(2)}) %collective-permute-start.1) | collective-permute-done | bytes 131104 | tf_op jit(solution)/shard_map/ppermute | solution.py:281
  75.7 11.4 %all_to_all.21.pair_ref = bf16[8,2,32,128]{3,2,1,0:T(8,128)(2,1)S(1)} all-to-all(bf16[8,2,32,128]{3,2,1,0:T(8,128)(2,1)S(1)} %add.1), channel_id=1, replica_groups=mesh['ctx'=64,'head'=8] {'head'}, dimensions={0} | all-to-all | bytes 262144 | tf_op jit(solution)/shard_map/all_to_all | solution.py:284
  87.1 0.8 unpack.1
  (3 shorter events, 0.0 us)
Async XLA Ops:
  0.6 33.6 %copy-start.2 = (f32[16,256]{1,0:T(8,128)S(1)}, f32[16,256]{1,0:T(8,128)}, u32[]{:S(2)}) copy-start(f32[16,256]{1,0:T(8,128)} %ln_ref.5) | copy-start | bytes 49156
  0.6 33.6 %copy-start.3 = (f32[16,256]{1,0:T(8,128)S(1)}, f32[16,256]{1,0:T(8,128)}, u32[]{:S(2)}) copy-start(f32[16,256]{1,0:T(8,128)} %dl_ref.5) | copy-start | bytes 49156
  1.7 32.5 %copy-start = (bf16[256,2048]{1,0:T(8,128)(2,1)S(1)}, bf16[256,2048]{1,0:T(8,128)(2,1)}, u32[]{:S(2)}) copy-start(bf16[256,2048]{1,0:T(8,128)(2,1)} %q_ref.5) | copy-start | bytes 3145732
  1.7 32.5 %copy-start.1 = (bf16[256,2048]{1,0:T(8,128)(2,1)S(1)}, bf16[256,2048]{1,0:T(8,128)(2,1)}, u32[]{:S(2)}) copy-start(bf16[256,2048]{1,0:T(8,128)(2,1)} %do_ref.5) | copy-start | bytes 3145732
  15.7 13.4 %collective-permute-start = (bf16[8,2,32,128]{3,2,1,0:T(8,128)(2,1)S(1)}, bf16[8,2,32,128]{3,2,1,0:T(8,128)(2,1)S(1)}, u32[]{:S(2)}, u32[]{:S(2)}) collective-permute-start(bf16[8,2,32,128]{3,2,1,0:T(8,128)(2,1)S(1)} %all_to_all.20.own_ref), channel_id=1, source_target_pairs={{0,32},{8,40},{16,48},{24,56},{32,64},{40,72},{48,80},{56,88},{64,... | collective-permute-start | bytes 393224 | tf_op jit(solution)/shard_map/ppermute | solution.py:258
  29.9 12.4 %all-to-all-start.1 = ((bf16[4,8,2,32,128]{4,3,2,1,0:T(8,128)(2,1)}), bf16[4,8,2,32,128]{4,3,2,1,0:T(8,128)(2,1)S(1)}, u32[]{:S(2)}, u32[]{:S(2)}) async-start(bf16[4,8,2,32,128]{4,3,2,1,0:T(8,128)(2,1)} %fill.1), calls=%async_computation.1 | async-start | bytes 1048576 | tf_op jit(solution)/shard_map/all_to_all | solution.py:263
  51.8 11.5 %all-to-all-start.2 = ((bf16[4,8,2,32,128]{4,3,2,1,0:T(8,128)(2,1)}), bf16[4,8,2,32,128]{4,3,2,1,0:T(8,128)(2,1)S(1)}, u32[]{:S(2)}, u32[]{:S(2)}) async-start(bf16[4,8,2,32,128]{4,3,2,1,0:T(8,128)(2,1)} %get-tuple-element.26), calls=%async_computation.2 | async-start | bytes 1048576 | tf_op jit(solution)/shard_map/all_to_all | solution.py:269
  63.4 12.2 %collective-permute-start.1 = (bf16[8,2,32,128]{3,2,1,0:T(8,128)(2,1)S(1)}, bf16[8,2,32,128]{3,2,1,0:T(8,128)(2,1)S(1)}, u32[]{:S(2)}, u32[]{:S(2)}) collective-permute-start(bf16[8,2,32,128]{3,2,1,0:T(8,128)(2,1)S(1)} %prev_sum.1), channel_id=1, source_target_pairs={{32,0},{40,8},{48,16},{56,24},{64,32},{72,40},{80,48},{88,56},{96,... | collective-permute-start | bytes 393224 | tf_op jit(solution)/shard_map/ppermute | solution.py:281
